TPU v7x, 32 devices: a whole 2x2x4 slice. The times are simulated.
32 devices in a mesh: member: 2 (over x), tile: 16 (over z, y, core).
Axes of the slice: x: 2, y: 2, z: 4, core: 2. Of those that a mesh axis runs over, the one named last changes fastest.
Arguments:
- parent_state: float32 [5, 8, 384, 768], P(None, None, ('member', 'tile')), parts along dimension 2, may hold values from -6 to 6
- nest_state: float32 [32, 5, 8, 36, 144], P(('member', 'tile')), parts along dimension 0, may hold values from -6 to 6
- metrics: float32 [3, 192, 768], P(None, 'tile'), may hold values from 0.5 to 2
- wave_speed: float32 [8], replicated, may hold values from 0.05 to 0.2
- nest_patch: int32 [16], replicated, may hold values from 0 to 255, as said below
Outputs:
- parent_next: float32 [5, 8, 384, 768], P(None, None, ('member', 'tile')), parts along dimension 2
- nest_next: float32 [32, 5, 8, 36, 144], P(('member', 'tile')), parts along dimension 0
There are 2 independent parts, one for each index of `member`. A program takes and returns all parts, laid end to end along the dimension named above; an argument that names none is the same for every part. Nothing has to cross between parts.
Inputs may be any that keep to these rules, and one draw needn't show every extreme that they name: Every device index d equals nest_patch[b] // 16 for exactly one nest block b.
All inputs are finite; a program needn't handle non-finite values.
Results may differ from a plain program's by a relative error of at most 0.0003.
Values sent between devices are 32-bit elements; how exact they have to be, the bound alone decides.
No kernel may reach another device: no remote copies, remote signals or barrier semaphores. Data moves between devices by JAX's collectives and lax.ppermute only.
A program may use at most 128 MiB of HBM per device.

v0:
```python
import jax
import jax.numpy as jnp
from jax import lax
from jax.sharding import PartitionSpec as P

PBX = 12
PBY = 48
NSTEP = 4


DIFFUSION = 0.1


def padded(block, sides, width):
    for axis, dim in sides:
        count = lax.axis_size(axis)
        forward = [(i, i + 1) for i in range(count - 1)]
        forward.append((count - 1, 0))
        backward = [(target, source) for source, target in forward]
        low = lax.ppermute(
            lax.slice_in_dim(block, block.shape[dim] - width, None, axis=dim), axis, forward
        )
        high = lax.ppermute(lax.slice_in_dim(block, 0, width, axis=dim), axis, backward)
        block = jnp.concatenate([low, block, high], axis=dim)
    return block


def stencil(centre, eastern, western, northern, southern, metrics, speeds):
    spread = eastern + western + northern + southern - 4.0 * centre
    across_x = metrics[0]
    across_y = metrics[1]
    per_area = metrics[2]
    height = (
        centre[0]
        - speeds * per_area * (centre[1] - western[1] + (centre[2] - southern[2]))
        + DIFFUSION * spread[0]
    )
    zonal_wind = centre[1] - speeds * across_x * (eastern[0] - centre[0]) + DIFFUSION * spread[1]
    merid_wind = centre[2] - speeds * across_y * (northern[0] - centre[0]) + DIFFUSION * spread[2]
    thermal = (
        centre[3]
        - 0.5
        * speeds
        * (
            centre[1] * (eastern[3] - western[3]) * across_x
            + centre[2] * (northern[3] - southern[3]) * across_y
        )
        + DIFFUSION * spread[3]
    )
    vertical = centre[4] + speeds * (centre[3] - centre[0]) + DIFFUSION * spread[4]
    return jnp.stack([height, zonal_wind, merid_wind, thermal, vertical])


def parent_advance(extended, metrics, speeds):
    centre = extended[..., 1:-1, :]
    eastern = extended[..., 2:, :]
    western = extended[..., :-2, :]
    northern = jnp.roll(centre, -1, axis=-1)
    southern = jnp.roll(centre, 1, axis=-1)
    return stencil(centre, eastern, western, northern, southern, metrics, speeds)


def wrap_columns(field):
    return jnp.concatenate([field[..., -1:], field, field[..., :1]], axis=-1)


def nest_run(state, coarse, coarse_metrics, speeds):
    fine_metrics = jnp.repeat(jnp.repeat(coarse_metrics, 3, axis=-2), 3, axis=-1)
    top_line = jnp.repeat(coarse[..., 0, 1:-1], 3, axis=-1)[..., None, :]
    bottom_line = jnp.repeat(coarse[..., -1, 1:-1], 3, axis=-1)[..., None, :]
    left_line = jnp.repeat(coarse[..., 1:-1, 0], 3, axis=-1)[..., None]
    right_line = jnp.repeat(coarse[..., 1:-1, -1], 3, axis=-1)[..., None]

    def one_step(index, current):
        eastern = jnp.concatenate([current[..., 1:, :], bottom_line], axis=-2)
        western = jnp.concatenate([top_line, current[..., :-1, :]], axis=-2)
        northern = jnp.concatenate([current[..., 1:], right_line], axis=-1)
        southern = jnp.concatenate([left_line, current[..., :-1]], axis=-1)
        return stencil(current, eastern, western, northern, southern, fine_metrics, speeds)

    return lax.fori_loop(0, 3 * NSTEP, one_step, state)


def coarsen(state):
    shaped = state.reshape(state.shape[:-2] + (state.shape[-2] // 3, 3, state.shape[-1] // 3, 3))
    return jnp.sum(shaped, axis=(-3, -1)) * (1.0 / 9.0)


def select_row(wanted, pieces):
    extent = pieces[0].shape[0]
    inside = (wanted >= 0) & (wanted < extent)
    safe = jnp.clip(wanted, 0, extent - 1)
    return tuple(
        (
            jnp.where(inside, lax.dynamic_index_in_dim(piece, safe, 0, keepdims=False), 0.0)
            for piece in pieces
        )
    )


def body(parent_state, nest_state, metrics, wave_speed, nest_patch):
    me = lax.axis_index("tile")
    count = lax.axis_size("tile")
    rows_dev = parent_state.shape[2]
    columns = parent_state.shape[3]
    speeds = wave_speed[:, None, None]
    patches_y = columns // PBY
    per_device = rows_dev // PBX * patches_y
    hosts = nest_patch // per_device
    order = jnp.arange(count, dtype=jnp.int32)
    hosted_block = jnp.sum(jnp.where(hosts == me, order, 0))
    my_host = hosts[me]
    local = nest_patch[hosted_block] - me * per_device
    row_first = local // patches_y * PBX
    col_first = local % patches_y * PBY
    extended = padded(parent_state, (("tile", 2),), NSTEP)
    wide_metrics = padded(metrics, (("tile", 1),), NSTEP)
    rim_rows = extended[:, :, NSTEP - 1 : extended.shape[2] - NSTEP + 1]
    state = extended
    for step in range(NSTEP):
        state = parent_advance(
            state, wide_metrics[:, step + 1 : wide_metrics.shape[1] - step - 1], speeds
        )
    coarse = lax.dynamic_slice_in_dim(wrap_columns(rim_rows), col_first, PBY + 2, 3)
    coarse_metrics = lax.dynamic_slice(metrics, (0, row_first, col_first), (3, PBX, PBY))
    got_coarse, got_metrics = select_row(
        my_host,
        (
            lax.all_gather(coarse[None], "tile", axis=0, tiled=True),
            lax.all_gather(coarse_metrics[None], "tile", axis=0, tiled=True),
        ),
    )
    final = nest_run(nest_state[0], got_coarse, got_metrics, speeds)
    average = coarsen(final)
    returned = select_row(
        hosted_block, (lax.all_gather(average[None], "tile", axis=0, tiled=True),)
    )[0]
    parent_next = lax.dynamic_update_slice(state, returned, (0, 0, row_first, col_first))
    return (parent_next, final[None])


def solution(mesh):
    in_specs = (
        P(None, None, ("member", "tile"), None),
        P(("member", "tile"), None, None, None, None),
        P(None, "tile", None),
        P(),
        P(),
    )
    out_specs = (
        P(None, None, ("member", "tile"), None),
        P(("member", "tile"), None, None, None, None),
    )
    return jax.shard_map(body, mesh=mesh, in_specs=in_specs, out_specs=out_specs, check_vma=False)
```

profile of v0, /device:TPU:1, one launch (start us, length us, event | category | flops | bytes accessed | tf_op | source)
XLA Modules:
  0.0 328.4 jit_solution(4219129621138966925)
XLA Ops:
  8.2 2.7 collective-permute-start.2
  10.9 2.2 fusion.200
  13.1 2.9 collective-permute-start.1
  22.7 21.0 %all-gather = f32[48,12,48]{2,1,0:T(8,128)S(1)} all-gather(f32[3,12,48]{2,1,0:T(8,128)S(1)} %constant_dynamic-slice_fusion), channel_id=2, replica_groups=mesh['member'=2,'tile'=16] {'tile'}, dimensions={0}, use_global_device_ids=true | all-gather | bytes 117504 | tf_op jit(solution)/shard_map/all_gather | solution.py:130
  45.9 1.8 copy.74
  51.2 2.8 fusion.192
  55.1 5.3 %fusion.52 = f32[5,8,18,768]{3,1,2,0:T(8,128)S(1)} fusion(f32[5,8,18,1]{3,1,2,0:T(8,128)S(1)} %get-tuple-element.162, f32[5,8,18,1]{3,1,2,0:T(8,128)S(1)} %get-tuple-element.161, f32[5,8,20,768]{3,1,2,0:T(8,128)} %copy-done, f32[5,8,18,767]{3,1,2,0:T(8,128)} %get-tuple-element.160, f32[5,8,18,767]{3,1,2,0:T(8,128)} %get-tuple-element.159), kind=kLoop, calls=%fused_computation.101 | loop fusion | flops 3870720 | bytes 13271040 | tf_op jit(solution)/shard_map/sub | solution.py:29
  61.3 1.4 copy-done.3
  72.2 32.7 %all-gather.6.cloned.1.call-done = f32[80,8,14,50]{3,1,2,0:T(8,128)} async-done(((f32[5,8,14,50]{3,1,2,0:T(8,128)}), f32[80,8,14,50]{3,1,2,0:T(8,128)}) %all-gather.6.cloned.1.call-update) | async-done | bytes 1792016 | tf_op jit(solution)/shard_map/all_gather | solution.py:129
  107.4 105.6 %while.11 = (s32[]{:T(128)}, f32[5,8,36,144]{3,2,1,0:T(8,128)S(1)}, f32[8,1,1]{0,2,1:T(1,128)S(1)}, f32[3,36,144]{2,1,0:T(8,128)S(1)}, f32[5,8,48]{1,2,0:T(8,128...) while((s32[]{:T(128)}, f32[5,8,36,144]{3,2,1,0:T(8,128)S(1)}, ...), condition=%wide.region_2.3_spmd.clone, body=%wide.region_1.2_spmd.clone.sunk | while | flops 3691017 | bytes 35468016 | solution.py:81
  180.2 1.2 copy.80
  213.1 7.1 %copy.67 = f32[5,8,36,144]{1,3,2,0:T(8,128)} copy(f32[5,8,36,144]{3,2,1,0:T(8,128)S(1)} %get-tuple-element.44) | data formatting | bytes 1658880 | tf_op jit(solution)/shard_map/while | solution.py:81
  220.1 20.6 %reshape.95 = f32[5,8,12,3,48,3]{1,5,4,3,2,0:T(4,128)} reshape(f32[5,8,36,144]{1,3,2,0:T(8,128)} %copy.67) | data formatting | bytes 1658880 | tf_op jit(solution)/shard_map/reshape | solution.py:85
  240.7 18.1 %reduce_sum.19 = f32[5,8,12,48]{1,3,2,0:T(8,128)} reduce(f32[5,8,12,3,48,3]{1,5,4,3,2,0:T(4,128)} %reshape.95, f32[]{:T(128)} %constant.93.clone.1), dimensions={3,5}, to_apply=%region_3.4 | reduce | flops 184320 | bytes 921604 | tf_op jit(solution)/shard_map/reduce_sum | solution.py:86
  258.8 2.6 copy.68
  261.4 1.7 broadcast_multiply_fusion.1
  263.2 2.3 constant_dynamic-update-slice_fusion.15
  265.5 2.1 constant_dynamic-update-slice_fusion.14
  267.6 1.8 constant_dynamic-update-slice_fusion.13
  270.6 2.3 fusion.198
  273.0 3.2 fusion.61
  277.7 1.6 copy.75
  279.2 31.3 %all-gather.8.cloned.1.call-done = f32[80,8,12,48]{3,1,2,0:T(8,128)} async-done(((f32[5,8,12,48]{3,1,2,0:T(8,128)}), f32[80,8,12,48]{3,1,2,0:T(8,128)}) %all-gather.8.cloned.1.call-update) | async-done | bytes 1474576 | tf_op jit(solution)/shard_map/all_gather | solution.py:136
  311.5 8.9 %dynamic_update_slice.4 = f32[5,8,12,768]{3,1,2,0:T(8,128)S(1)} dynamic-update-slice(f32[5,8,12,768]{3,1,2,0:T(8,128)S(1)} %fusion.164, f32[5,8,12,48]{3,1,2,0:T(8,128)S(1)} %select_bitcast_fusion.1, s32[]{:T(128)} %constant.82.clone.1, s32[]{:T(128)} %constant.82.clone.1, s32[]{:T(128)} %constant.82.clone.1, s32[]{:T(128)S(6)} %select_n.79) | dynamic-update-slice | bytes 184324 | tf_op jit(solution)/shard_map/dynamic_update_slice | solution.py:138
  (673 shorter events, 127.6 us)
Async XLA Ops:
  7.2 14.2 %copy-start.35 = (f32[3,12,768]{2,1,0:T(8,128)S(1)}, f32[3,12,768]{2,1,0:T(8,128)}, u32[]{:S(2)}) copy-start(f32[3,12,768]{2,1,0:T(8,128)} %param.9) | copy-start | bytes 331780
  7.2 8.9 %copy-start.44 = (s32[16]{0:T(128)S(1)}, s32[16]{0:T(128)}, u32[]{:S(2)}) copy-start(s32[16]{0:T(128)} %param.11) | copy-start | bytes 196
  7.2 14.8 %copy-start.36 = (f32[8]{0:T(128)S(1)}, f32[8]{0:T(128)}, u32[]{:S(2)}) copy-start(f32[8]{0:T(128)} %param.10) | copy-start | bytes 100
  7.2 97.8 %all-gather.6.cloned.1.call-start = ((), (), s32[]{:S(2)}) async-start(), calls=%async_computation | async-start | bytes 4874240 | tf_op jit(solution)/shard_map/all_gather | solution.py:129
  8.2 39.6 %collective-permute-start.2 = (f32[3,4,768]{2,1,0:T(4,128)S(1)}, f32[3,4,768]{2,1,0:T(4,128)S(1)}, u32[]{:S(2)}, u32[]{:S(2)}) collective-permute-start(f32[3,4,768]{2,1,0:T(4,128)S(1)} %get-tuple-element.193), channel_id=1, source_target_pairs={{0,1},{1,2},{2,3},{3,4},{4,5},{5,6},{6,7},{7,8},{8,9},{9,10},{10,1... | collective-permute-start | bytes 110600 | tf_op jit(solution)/shard_map/ppermute | solution.py:20
  10.9 36.9 %collective-permute-start.3 = (f32[3,4,768]{2,1,0:T(4,128)S(1)}, f32[3,4,768]{2,1,0:T(4,128)S(1)}, u32[]{:S(2)}, u32[]{:S(2)}) collective-permute-start(f32[3,4,768]{2,1,0:T(4,128)S(1)} %get-tuple-element.194), channel_id=1, source_target_pairs={{1,0},{2,1},{3,2},{4,3},{5,4},{6,5},{7,6},{8,7},{9,8},{10,9},{11,1... | collective-permute-start | bytes 110600 | tf_op jit(solution)/shard_map/ppermute | solution.py:23
  13.1 36.6 %collective-permute-start.1 = (f32[5,8,4,768]{3,1,2,0:T(8,128)}, f32[5,8,4,768]{3,1,2,0:T(8,128)S(1)}, u32[]{:S(2)}, u32[]{:S(2)}) collective-permute-start(f32[5,8,4,768]{3,1,2,0:T(8,128)} %get-tuple-element.175), channel_id=1, source_target_pairs={{1,0},{2,1},{3,2},{4,3},{5,4},{6,5},{7,6},{8,7},{9,8},{10,9},{11,1... | collective-permute-start | bytes 1474568 | tf_op jit(solution)/shard_map/ppermute | solution.py:23
  16.0 32.5 %collective-permute-start = (f32[5,8,4,768]{3,1,2,0:T(8,128)}, f32[5,8,4,768]{3,1,2,0:T(8,128)}, u32[]{:S(2)}, u32[]{:S(2)}) collective-permute-start(f32[5,8,4,768]{3,1,2,0:T(8,128)} %get-tuple-element.176), channel_id=1, source_target_pairs={{0,1},{1,2},{2,3},{3,4},{4,5},{5,6},{6,7},{7,8},{8,9},{9,10},{10,1... | collective-permute-start | bytes 1474568 | tf_op jit(solution)/shard_map/ppermute | solution.py:20
  48.5 22.7 %copy-start.40 = (f32[14,768]{1,0:T(8,128)}, f32[14,768]{1,0:T(8,128)S(1)}, u32[]{:S(2)}) copy-start(f32[14,768]{1,0:T(8,128)S(1)} %get-tuple-element.182) | copy-start | bytes 129028
  55.0 255.6 %all-gather.8.cloned.1.call-start = ((), (), s32[]{:S(2)}) async-start(), calls=%async_computation.1 | async-start | bytes 4177920 | tf_op jit(solution)/shard_map/all_gather | solution.py:136
  55.1 5.3 %copy-start.1 = (f32[5,8,20,768]{3,1,2,0:T(8,128)S(1)}, f32[5,8,20,768]{3,1,2,0:T(8,128)}, u32[]{:S(2)}) copy-start(f32[5,8,20,768]{3,1,2,0:T(8,128)} %copy-done) | copy-start | bytes 7372804
  55.1 5.8 %copy-start.2 = (f32[5,8,18,767]{3,1,2,0:T(8,128)S(1)}, f32[5,8,18,767]{3,1,2,0:T(8,128)}, u32[]{:S(2)}) copy-start(f32[5,8,18,767]{3,1,2,0:T(8,128)} %get-tuple-element.160) | copy-start | bytes 6626884
  65.2 5.9 %copy-start.8 = (f32[1,8,16,768]{3,1,2,0:T(8,128)}, f32[1,8,16,768]{3,1,2,0:T(8,128)S(1)}, u32[]{:S(2)}) copy-start(f32[1,8,16,768]{3,1,2,0:T(8,128)S(1)} %get-tuple-element.139) | copy-start | bytes 1179652
  65.4 5.7 %copy-start.12 = (f32[1,8,16,768]{3,1,2,0:T(8,128)}, f32[1,8,16,768]{3,1,2,0:T(8,128)S(1)}, u32[]{:S(2)}) copy-start(f32[1,8,16,768]{3,1,2,0:T(8,128)S(1)} %get-tuple-element.137) | copy-start | bytes 1179652
  65.6 3.9 %copy-start.16 = (f32[1,8,16,768]{3,1,2,0:T(8,128)}, f32[1,8,16,768]{3,1,2,0:T(8,128)S(1)}, u32[]{:S(2)}) copy-start(f32[1,8,16,768]{3,1,2,0:T(8,128)S(1)} %get-tuple-element.135) | copy-start | bytes 1179652
  258.8 4.3 %copy-start.5 = (f32[5,8,14,767]{3,1,2,0:T(8,128)S(1)}, f32[5,8,14,767]{3,1,2,0:T(8,128)}, u32[]{:S(2)}) copy-start(f32[5,8,14,767]{3,1,2,0:T(8,128)} %copy-done.4) | copy-start | bytes 5154244
  258.8 4.3 %copy-start.37 = (f32[14,768]{1,0:T(8,128)S(1)}, f32[14,768]{1,0:T(8,128)}, u32[]{:S(2)}) copy-start(f32[14,768]{1,0:T(8,128)} %get-tuple-element.181) | copy-start | bytes 129028
  263.1 2.3 copy-start.7
  263.1 2.3 copy-start.11
  263.1 2.3 copy-start.13
  263.1 2.3 copy-start.17
  273.0 3.2 copy-start.10
  273.0 3.2 copy-start.15
  273.0 3.2 copy-start.42
  (148 other events, 167.9 us)
Sparse Core Ops, SparseCore 0:
  55.1 49.7 all-gather.5
  263.2 47.3 all-gather.7
where the time goes:
time: 330 us; the launch traced here: 328 us
  local copies, waits for them, and re-layouts  144 us (44%)
  other arithmetic  70.3 us (21%)
  waiting for transfers between devices  64.1 us (19%)
  blocking collectives  21 us (6%)
  between operations  20.5 us (6%)
  starting transfers between devices  5.7 us (2%)
    all_gather x1, waiting for transfers between devices, body(): lax.all_gather(coarse[None], 'tile', axis=0, tiled=True)  32.7 us
    all_gather x1, waiting for transfers between devices, body(): lax.all_gather(average[None], 'tile', axis=0, tiled=True)  31.3 us
    sub x16, other arithmetic, stencil(): spread = eastern + western + northern + southern - 4.0 * centre  23 us
    all_gather x1, blocking collectives, body(): lax.all_gather(coarse_metrics[None], 'tile', axis=0, tiled=True)  21 us
    reshape x1, local copies, waits for them, and re-layouts, coarsen(): state.reshape(state.shape[:-2] + (state.shape[-2] // 3, 3, state.shape[-1...  20.6 us
    while x276, local copies, waits for them, and re-layouts  18.2 us
    reduce_sum x1, other arithmetic, coarsen(): return jnp.sum(shaped, axis=(-3, -1)) * (1.0 / 9.0)  18.1 us
    another operation x24, local copies, waits for them, and re-layouts, nest_run(): left_line = jnp.repeat(coarse[..., 1:-1, 0], 3, axis=-1)[..., None]  15.5 us
  transfers between devices with their start and end apart: 6, of which 2 were waited for; matrix products, arithmetic and copies ran while one was open for 12% of the time, Pallas kernels for 0%

commit v1 on v0

v1 whole, which is shorter than its diff:
```python
import functools

import jax
import jax.numpy as jnp
from jax import lax
from jax.experimental import pallas as pl
from jax.experimental.pallas import tpu as pltpu
from jax.sharding import PartitionSpec as P

PBX = 12
PBY = 48
NSTEP = 4
DIFFUSION = 0.1

FIELDS = 5
LEVELS = 8
FX = 3 * PBX
FY = 3 * PBY
LANES = 128
GROUPS = 16
COLS = FY // GROUPS
ROWS = 5
SLOT = 24
META = 8
F32 = jnp.float32
BF16 = jnp.bfloat16
VMEM = pl.BlockSpec(memory_space=pltpu.VMEM)
SMEM = pl.BlockSpec(memory_space=pltpu.SMEM)
ANY = pl.BlockSpec(memory_space=pl.ANY)


def params():
    return pltpu.CompilerParams(vmem_limit_bytes=40 * 1024 * 1024)


def cost(flops, moved):
    return pl.CostEstimate(flops=flops, bytes_accessed=moved, transcendentals=0)


def iota(shape, dim):
    return lax.broadcasted_iota(jnp.int32, shape, dim)


def chooser(mask):
    return jnp.where(mask, 1.0, 0.0).astype(BF16)


def pick(values, matrix, terms):
    total = None
    for term in range(terms):
        part = values.astype(BF16)
        piece = jnp.dot(part, matrix, preferred_element_type=F32)
        total = piece if total is None else total + piece
        if term + 1 < terms:
            values = values - part.astype(F32)
    return total


def level_speeds(speed_ref, index):
    speeds = jnp.zeros(index.shape, F32)
    for level in range(LEVELS):
        speeds = jnp.where(index == level, speed_ref[level], speeds)
    return speeds


def prepare_kernel(
    per_device, patch_ref, parent_ref, metrics_ref, meta_ref, slots_ref, up_ref, down_ref, lines_ref, cells_ref
):
    count = patch_ref.shape[0]
    columns = parent_ref.shape[3]
    rows = parent_ref.shape[2]
    me = lax.axis_index("tile")

    def note(block, carry):
        meta_ref[META + patch_ref[block] // per_device] = block
        return carry

    lax.fori_loop(0, count, note, 0)
    own = meta_ref[META + me]
    after = meta_ref[META + lax.rem(me + 1, count)]
    before = meta_ref[META + lax.rem(me + count - 1, count)]
    meta_ref[0] = patch_ref[me] // per_device
    meta_ref[1] = lax.rem(patch_ref[own], per_device) * PBY
    last_window = columns - 2 * LANES

    def place(block):
        first = lax.rem(patch_ref[block], per_device) * PBY
        window = jnp.minimum(first // LANES * LANES, last_window)
        return first, pl.multiple_of(window, LANES)

    def window_matrix(offset):
        source = iota((2 * LANES, LANES), 0)
        lane = iota((2 * LANES, LANES), 1)
        wanted = offset + 3 * lax.rem(lane, GROUPS) + lane // GROUPS
        return chooser((source == wanted) & (lane < PBY))

    first, window = place(own)
    for kind in range(3):
        cells_ref[pl.ds(kind * 16, PBX), :] = metrics_ref[kind, :, pl.ds(window, 2 * LANES)]
    mets = pick(cells_ref[...], window_matrix(first - window), 3)
    mets = [mets[kind * 16 : kind * 16 + PBX] for kind in range(3)]
    lane = iota((PBX, LANES), 1)
    packed = jnp.where(
        lane < PBY,
        mets[0],
        jnp.where(lane < 2 * PBY, pltpu.roll(mets[1], PBY, 1), pltpu.roll(mets[2], 2 * PBY, 1)),
    )
    edges = pltpu.roll(mets[2], 48, 1)
    left = lax.rem(first + columns - 1, columns)
    right = lax.rem(first + PBY, columns)
    for side, column in enumerate((left, right)):
        block = pl.multiple_of(column // LANES * LANES, LANES)
        spot = lax.rem(column, LANES)
        for field in range(FIELDS):
            for level in range(LEVELS):
                target = 2 * (field * LEVELS + level) + side
                strip = parent_ref[field, level, :, pl.ds(block, LANES)]
                strip = pltpu.roll(strip, lax.rem(target - spot + LANES, LANES), 1)
                edges = jnp.where(lane == target, strip, edges)
    slots_ref[own, pl.ds(0, PBX), :] = edges
    slots_ref[own, pl.ds(PBX, PBX), :] = packed

    sub8 = iota((LEVELS, LANES), 0)
    chunk8 = iota((LEVELS, LANES), 1) // GROUPS
    for block, row in ((after, rows - 1), (before, 0)):
        first, window = place(block)
        for field in range(FIELDS):
            for level in range(LEVELS):
                lines_ref[pl.ds(field * LEVELS + level, 1), :] = parent_ref[
                    field, level, pl.ds(row, 1), pl.ds(window, 2 * LANES)
                ]
        found = pick(lines_ref[...], window_matrix(first - window), 3)
        for field in range(FIELDS):
            values = found[field * LEVELS : (field + 1) * LEVELS]
            for third in range(3):
                turned = pltpu.roll(values, LANES - GROUPS * third, 1) if third else values
                turned = pltpu.roll(turned, 0, 1, stride=GROUPS, stride_axis=0)
                line = jnp.sum(jnp.where(chunk8 == sub8, turned, 0.0), axis=0, keepdims=True)
                slots_ref[block, pl.ds(field * 3 + third, 1), :] = line

    for field in range(FIELDS):
        for level in range(LEVELS):
            up_ref[field * LEVELS + level] = parent_ref[field, level, pl.ds(rows - NSTEP, NSTEP), :]
            down_ref[field * LEVELS + level] = parent_ref[field, level, pl.ds(0, NSTEP), :]
    for kind in range(3):
        up_ref[FIELDS * LEVELS + kind] = metrics_ref[kind, pl.ds(rows - NSTEP, NSTEP), :]
        down_ref[FIELDS * LEVELS + kind] = metrics_ref[kind, pl.ds(0, NSTEP), :]


def prepare(nest_patch, parent_state, metrics, per_device):
    count = nest_patch.shape[0]
    columns = parent_state.shape[3]
    halo = jax.ShapeDtypeStruct((FIELDS * LEVELS + 3, NSTEP, columns), F32)
    return pl.pallas_call(
        functools.partial(prepare_kernel, per_device),
        out_shape=(
            jax.ShapeDtypeStruct((META + count,), jnp.int32),
            jax.ShapeDtypeStruct((count, SLOT, LANES), F32),
            halo,
            halo,
        ),
        in_specs=[SMEM, VMEM, VMEM],
        out_specs=(SMEM, VMEM, VMEM, VMEM),
        scratch_shapes=[
            pltpu.VMEM((FIELDS * LEVELS, 2 * LANES), F32),
            pltpu.VMEM((48, 2 * LANES), F32),
        ],
        compiler_params=params(),
        cost_estimate=cost(4_000_000, 4_000_000),
        name="prepare",
    )(nest_patch, parent_state, metrics)


def swap_chunks(parts):
    chunk = iota((8, LANES), 1) // GROUPS
    parts = list(parts)
    for bit in (1, 2, 4):
        high = (chunk & bit) != 0
        for low_index in range(8):
            if low_index & bit:
                continue
            high_index = low_index | bit
            low_part, high_part = parts[low_index], parts[high_index]
            parts[low_index] = jnp.where(high, pltpu.roll(high_part, GROUPS * bit, 1), low_part)
            parts[high_index] = jnp.where(
                high, high_part, pltpu.roll(low_part, LANES - GROUPS * bit, 1)
            )
    return parts


def column_order(shape, natural_dim):
    natural = iota(shape, natural_dim)
    packed = iota(shape, 1 - natural_dim)
    return chooser(
        (natural == COLS * lax.rem(packed, GROUPS) + packed // GROUPS) & (packed < FY)
    )


HEIGHT = 40


def nest_in_kernel(nest_ref, out_ref, plain_ref, mixed_ref):
    order = column_order((FY, 2 * LANES), 0)
    for level in range(LEVELS):
        plain_ref[pl.ds(level * HEIGHT + 32, 8), :] = jnp.zeros((8, FY), F32)

    def one_field(field, carry):
        for level in range(LEVELS):
            plain_ref[pl.ds(level * HEIGHT, FX), :] = nest_ref[0, field, level]
        mixed = pick(plain_ref[...], order, 2)
        mixed_ref[0] = mixed[:, :LANES]
        mixed_ref[1] = mixed[:, LANES:]
        for row in range(ROWS):
            parts = [
                mixed_ref[0, pl.ds(level * HEIGHT + row, 8, stride=ROWS), :]
                for level in range(LEVELS)
            ]
            extra = mixed_ref[1, pl.ds(row, 8, stride=ROWS), :]
            for level in range(1, LEVELS):
                extra = extra + pltpu.roll(
                    mixed_ref[1, pl.ds(level * HEIGHT + row, 8, stride=ROWS), :],
                    GROUPS * level,
                    1,
                )
            parts = swap_chunks(parts) + [extra]
            for col in range(COLS):
                out_ref[field, col, row] = parts[col]
        return carry

    lax.fori_loop(0, FIELDS, one_field, 0)


PACKED = (FIELDS, COLS, ROWS, 8, LANES)


def nest_in(nest_state):
    return pl.pallas_call(
        nest_in_kernel,
        out_shape=jax.ShapeDtypeStruct(PACKED, F32),
        in_specs=[VMEM],
        out_specs=VMEM,
        scratch_shapes=[
            pltpu.VMEM((LEVELS * HEIGHT, FY), F32),
            pltpu.VMEM((2, LEVELS * HEIGHT, LANES), F32),
        ],
        compiler_params=params(),
        cost_estimate=cost(8_000_000, 6_000_000),
        name="nest_in",
    )(nest_state)


def nest_out_kernel(packed_ref, out_ref, mixed_ref):
    order = column_order((2 * LANES, FY), 1)
    few = iota((8, LANES), 1) < GROUPS

    def one_field(field, carry):
        for row in range(ROWS):
            parts = swap_chunks([packed_ref[field, col, row] for col in range(8)])
            extra = packed_ref[field, 8, row]
            for level in range(LEVELS):
                where = pl.ds(level * HEIGHT + row, 8, stride=ROWS)
                mixed_ref[0, where, :] = parts[level]
                turned = pltpu.roll(extra, LANES - GROUPS * level, 1) if level else extra
                mixed_ref[1, where, :] = jnp.where(few, turned, 0.0)
        mixed = jnp.concatenate([mixed_ref[0], mixed_ref[1]], axis=1)
        found = pick(mixed, order, 2)
        for level in range(LEVELS):
            out_ref[0, field, level] = found[level * HEIGHT : level * HEIGHT + FX]
        return carry

    lax.fori_loop(0, FIELDS, one_field, 0)


def nest_out(packed):
    return pl.pallas_call(
        nest_out_kernel,
        out_shape=jax.ShapeDtypeStruct((1, FIELDS, LEVELS, FX, FY), F32),
        in_specs=[VMEM],
        out_specs=VMEM,
        scratch_shapes=[pltpu.VMEM((2, LEVELS * HEIGHT, LANES), F32)],
        compiler_params=params(),
        cost_estimate=cost(8_000_000, 6_000_000),
        name="nest_out",
    )(packed)


def substep(centre, east, west, north, south, coef, speeds):
    by_area, by_x, by_y, half_x, half_y = coef
    spread = [
        (1.0 - 4.0 * DIFFUSION) * centre[f]
        + DIFFUSION * ((east[f] + west[f]) + (north[f] + south[f]))
        for f in range(FIELDS)
    ]
    height = spread[0] - by_area * ((centre[1] - west[1]) + (centre[2] - south[2]))
    zonal = spread[1] - by_x * (east[0] - centre[0])
    merid = spread[2] - by_y * (north[0] - centre[0])
    theta = spread[3] - (
        centre[1] * (east[3] - west[3]) * half_x + centre[2] * (north[3] - south[3]) * half_y
    )
    vertical = spread[4] + speeds * (centre[3] - centre[0])
    return height, zonal, merid, theta, vertical


def nest_kernel(
    meta_ref, speed_ref, recv_ref, start_ref, out_ref, mean_ref, a_ref, b_ref, coef_ref, rim_ref, sums_ref
):
    count = recv_ref.shape[0]
    host = meta_ref[0]
    lane = iota((8, LANES), 1)
    chunk = lane // GROUPS
    group = lax.rem(lane, GROUPS)
    sub = iota((8, LANES), 0)
    speeds = level_speeds(speed_ref, chunk)

    fine = iota((ROWS * 8, PBX), 0)
    coarse_row = jnp.minimum((ROWS * lax.rem(fine, 8) + fine // 8) // 3, PBX - 1)
    rows = chooser(coarse_row == iota((ROWS * 8, PBX), 1))
    source = recv_ref[host]
    both = jnp.concatenate([source[:PBX], source[PBX:]], axis=1)
    expanded = None
    for term in range(3):
        part = both.astype(BF16)
        piece = jnp.dot(rows, part, preferred_element_type=F32)
        expanded = piece if expanded is None else expanded + piece
        both = both - part.astype(F32)
    edges = expanded[:, :LANES]
    packed = expanded[:, LANES:]
    for row in range(ROWS):
        for index in range(9):
            if index < 8:
                piece = jnp.where(chunk == index, packed[row * 8 : row * 8 + 8], 0.0)
            else:
                piece = jnp.where(chunk == 5, edges[row * 8 : row * 8 + 8], 0.0)
            for shift in (64, 32, 16):
                piece = piece + pltpu.roll(piece, shift, 1)
            piece = piece * speeds
            kind, third = index // 3, index % 3
            if kind == 2:
                coef_ref[third, row, 0] = piece
            else:
                coef_ref[third, row, 1 + kind] = piece
                coef_ref[third, row, 3 + kind] = 0.5 * piece
    spot = iota((LANES, FIELDS * LANES), 0)
    target = iota((LANES, FIELDS * LANES), 1)
    inside = lax.rem(target, GROUPS)
    pair = 2 * (target // GROUPS)
    spread = chooser(
        ((inside == 0) & (spot == pair)) | ((inside == GROUPS - 1) & (spot == pair + 1))
    )
    rim = pick(edges, spread, 3)
    for row in range(ROWS):
        for field in range(FIELDS):
            rim_ref[field, row] = rim[row * 8 : row * 8 + 8, field * LANES : (field + 1) * LANES]

    top = recv_ref[lax.rem(host + count - 1, count), pl.ds(0, 15), :]
    bottom = recv_ref[lax.rem(host + 1, count), pl.ds(0, 15), :]

    def halo(ref, field):
        for row in range(ROWS):
            ref[field, 0, row] = jnp.where(
                group == 0, rim_ref[field, row], pltpu.roll(ref[field, COLS, row], 1, 1)
            )
            ref[field, COLS + 1, row] = jnp.where(
                group == GROUPS - 1,
                rim_ref[field, row],
                pltpu.roll(ref[field, 1, row], LANES - 1, 1),
            )

    for field in range(FIELDS):
        for col in range(COLS):
            index = field * 3 + col // 3
            for row in range(ROWS):
                value = start_ref[field, col, row]
                if row == 1:
                    value = jnp.where(sub == 7, bottom[index : index + 1], value)
                if row == 4:
                    value = jnp.where(sub == 7, top[index : index + 1], value)
                a_ref[field, col + 1, row] = value
        halo(a_ref, field)

    def one_step(src, dst):
        def thirds(third, carry):
            for inner in range(3):
                col = third * 3 + inner + 1
                centre = [[src[f, col, row] for f in range(FIELDS)] for row in range(ROWS)]
                below = [pltpu.roll(centre[ROWS - 1][f], 1, 0) for f in range(FIELDS)]
                above = [pltpu.roll(centre[0][f], 7, 0) for f in range(FIELDS)]
                for row in range(ROWS):
                    east = centre[row + 1] if row + 1 < ROWS else above
                    west = centre[row - 1] if row else below
                    north = [src[f, col + 1, row] for f in range(FIELDS)]
                    south = [src[f, col - 1, row] for f in range(FIELDS)]
                    coef = [coef_ref[third, row, k] for k in range(5)]
                    new = substep(centre[row], east, west, north, south, coef, speeds)
                    for f in range(FIELDS):
                        value = new[f]
                        if row in (1, 4):
                            value = jnp.where(sub == 7, centre[row][f], value)
                        dst[f, col, row] = value
            return carry

        lax.fori_loop(0, 3, thirds, 0)
        for field in range(FIELDS):
            halo(dst, field)

    def two_steps(index, carry):
        one_step(a_ref, b_ref)
        one_step(b_ref, a_ref)
        return carry

    lax.fori_loop(0, 3 * NSTEP // 2, two_steps, 0)

    for field in range(FIELDS):
        for third in range(3):
            index = field * 3 + third
            for row in range(ROWS):
                values = [a_ref[field, third * 3 + k + 1, row] for k in range(3)]
                for k in range(3):
                    out_ref[field, third * 3 + k, row] = values[k]
                sums_ref[pl.ds(index * HEIGHT + row, 8, stride=ROWS), :] = (
                    values[0] + values[1] + values[2]
                )
            total = sums_ref[pl.ds(index * HEIGHT, PBX, stride=3), :]
            for k in (1, 2):
                total = total + sums_ref[pl.ds(index * HEIGHT + k, PBX, stride=3), :]
            mean_ref[index] = total * (1.0 / 9.0)


def nest_run(meta, wave_speed, recv, start, pieces):
    padded = (FIELDS, COLS + 2, ROWS, 8, LANES)
    return pl.pallas_call(
        nest_kernel,
        out_shape=(
            jax.ShapeDtypeStruct(PACKED, F32),
            jax.ShapeDtypeStruct((pieces, PBX, LANES), F32),
        ),
        in_specs=[SMEM, SMEM, VMEM, VMEM],
        out_specs=(VMEM, VMEM),
        scratch_shapes=[
            pltpu.VMEM(padded, F32),
            pltpu.VMEM(padded, F32),
            pltpu.VMEM((3, ROWS, 5, 8, LANES), F32),
            pltpu.VMEM((FIELDS, ROWS, 8, LANES), F32),
            pltpu.VMEM((15 * HEIGHT, LANES), F32),
        ],
        compiler_params=params(),
        cost_estimate=cost(40_000_000, 3_000_000),
        name="nest_run",
    )(meta, wave_speed, recv, start)


def parent_kernel(speed_ref, parent_ref, low_ref, high_ref, metrics_ref, out_ref, a_ref, b_ref, wide_ref):
    rows = parent_ref.shape[2]
    columns = parent_ref.shape[3]
    parts = columns // LANES
    speeds = level_speeds(speed_ref, iota((LEVELS, columns), 0))
    for field in range(FIELDS):
        for level in range(LEVELS):
            index = field * LEVELS + level
            for part in range(parts):
                span = pl.ds(part * LANES, LANES)
                a_ref[field, part, pl.ds(level, NSTEP, stride=8), :] = low_ref[index, :, span]
                a_ref[field, part, pl.ds(NSTEP * 8 + level, rows, stride=8), :] = parent_ref[
                    field, level, :, span
                ]
                a_ref[field, part, pl.ds((NSTEP + rows) * 8 + level, NSTEP, stride=8), :] = (
                    high_ref[index, :, span]
                )
    for kind in range(3):
        wide_ref[kind, pl.ds(0, NSTEP), :] = low_ref[FIELDS * LEVELS + kind]
        wide_ref[kind, pl.ds(NSTEP, rows), :] = metrics_ref[kind]
        wide_ref[kind, pl.ds(NSTEP + rows, NSTEP), :] = high_ref[FIELDS * LEVELS + kind]

    def one_step(src, dst, first, last):
        def one_row(row, carry):
            def line(field, at):
                span = pl.ds(pl.multiple_of(at * 8, 8), 8)
                return jnp.concatenate([src[field, part, span, :] for part in range(parts)], axis=1)

            centre = [line(f, row) for f in range(FIELDS)]
            east = [line(f, row + 1) for f in range(FIELDS)]
            west = [line(f, row - 1) for f in range(FIELDS)]
            north = [pltpu.roll(centre[f], columns - 1, 1) for f in range(FIELDS)]
            south = [pltpu.roll(centre[f], 1, 1) for f in range(FIELDS)]
            met = [wide_ref[kind, pl.ds(row, 1), :] * speeds for kind in range(3)]
            coef = (met[2], met[0], met[1], 0.5 * met[0], 0.5 * met[1])
            new = substep(centre, east, west, north, south, coef, speeds)
            for f in range(FIELDS):
                for part in range(parts):
                    dst[f, part, pl.ds(pl.multiple_of(row * 8, 8), 8), :] = new[f][
                        :, part * LANES : (part + 1) * LANES
                    ]
            return carry

        lax.fori_loop(first, last, one_row, 0)

    refs = (a_ref, b_ref)
    for step in range(NSTEP):
        one_step(refs[step % 2], refs[(step + 1) % 2], step + 1, rows + 2 * NSTEP - 1 - step)
    final = refs[NSTEP % 2]
    for field in range(FIELDS):
        for level in range(LEVELS):
            for part in range(parts):
                out_ref[field, level, :, pl.ds(part * LANES, LANES)] = final[
                    field, part, pl.ds(NSTEP * 8 + level, rows, stride=8), :
                ]


def parent_run(wave_speed, parent_state, low, high, metrics):
    rows, columns = parent_state.shape[2:]
    wide = (FIELDS, columns // LANES, (rows + 2 * NSTEP) * 8, LANES)
    return pl.pallas_call(
        parent_kernel,
        out_shape=jax.ShapeDtypeStruct(parent_state.shape, F32),
        in_specs=[SMEM, VMEM, VMEM, VMEM, VMEM],
        out_specs=VMEM,
        scratch_shapes=[
            pltpu.VMEM(wide, F32),
            pltpu.VMEM(wide, F32),
            pltpu.VMEM((3, rows + 2 * NSTEP + 4, columns), F32),
        ],
        compiler_params=params(),
        cost_estimate=cost(40_000_000, 8_000_000),
        name="parent_run",
    )(wave_speed, parent_state, low, high, metrics)


def reorder_kernel(meta_ref, in_ref, out_ref):
    def one(index, carry):
        out_ref[index] = in_ref[meta_ref[META + index]]
        return carry

    lax.fori_loop(0, in_ref.shape[0], one, 0)


def reorder(meta, pieces):
    return pl.pallas_call(
        reorder_kernel,
        out_shape=jax.ShapeDtypeStruct(pieces.shape, F32),
        in_specs=[SMEM, VMEM],
        out_specs=VMEM,
        compiler_params=params(),
        cost_estimate=cost(100_000, 200_000),
        name="reorder",
    )(meta, pieces)


def insert_kernel(meta_ref, mean_ref, parent_ref, out_ref, rows_ref, window_ref, sem):
    columns = out_ref.shape[3]
    first = meta_ref[1]
    window = pl.multiple_of(
        jnp.minimum(first // LANES * LANES, columns - 2 * LANES), LANES
    )
    fetch = pltpu.make_async_copy(
        parent_ref.at[:, :, :, pl.ds(window, 2 * LANES)], window_ref, sem
    )
    fetch.start()
    offset = first - window
    lane = iota((PBX, LANES), 1)
    for field in range(FIELDS):
        thirds = [mean_ref[field * 3 + third] for third in range(3)]
        for level in range(LEVELS):
            turned = [
                pltpu.roll(thirds[third], (GROUPS * (third - level)) % LANES, 1)
                if third != level
                else thirds[third]
                for third in range(3)
            ]
            rows_ref[pl.ds((field * LEVELS + level) * 16, PBX), :] = jnp.where(
                lane < GROUPS,
                turned[0],
                jnp.where(lane < 2 * GROUPS, turned[1], jnp.where(lane < PBY, turned[2], 0.0)),
            )
    source = iota((LANES, 2 * LANES), 0)
    target = iota((LANES, 2 * LANES), 1)
    order = chooser(
        (target == offset + 3 * lax.rem(source, GROUPS) + source // GROUPS) & (source < PBY)
    )
    found = pick(rows_ref[...], order, 2)
    wide = iota((PBX, 2 * LANES), 1)
    inside = (wide >= offset) & (wide < offset + PBY)
    fetch.wait()
    for field in range(FIELDS):
        for level in range(LEVELS):
            at = (field * LEVELS + level) * 16
            window_ref[field, level] = jnp.where(
                inside, found[at : at + PBX], window_ref[field, level]
            )
    store = pltpu.make_async_copy(window_ref, out_ref.at[:, :, :, pl.ds(window, 2 * LANES)], sem)
    store.start()
    store.wait()


def insert(meta, means, advanced):
    rows = advanced.shape[2]
    return pl.pallas_call(
        insert_kernel,
        out_shape=jax.ShapeDtypeStruct(advanced.shape, F32),
        in_specs=[SMEM, VMEM, ANY],
        out_specs=ANY,
        scratch_shapes=[
            pltpu.VMEM((FIELDS * LEVELS * 16, LANES), F32),
            pltpu.VMEM((FIELDS, LEVELS, rows, 2 * LANES), F32),
            pltpu.SemaphoreType.DMA,
        ],
        input_output_aliases={2: 0},
        compiler_params=params(),
        cost_estimate=cost(4_000_000, 2_000_000),
        name="insert",
    )(meta, means, advanced)


def body(parent_state, nest_state, metrics, wave_speed, nest_patch):
    count = lax.axis_size("tile")
    rows, columns = parent_state.shape[2:]
    per_device = rows // PBX * (columns // PBY)
    forward = [(i, (i + 1) % count) for i in range(count)]
    backward = [(target, source) for source, target in forward]

    meta, slots, up, down = prepare(nest_patch, parent_state, metrics, per_device)
    recv = lax.all_to_all(slots, "tile", 0, 0, tiled=True)
    low = lax.ppermute(up, "tile", forward)
    high = lax.ppermute(down, "tile", backward)
    start = nest_in(nest_state)
    share = -(-15 * PBX // count)
    direct = share == PBX and count >= 15
    final, means = nest_run(meta, wave_speed, recv, start, count if direct else 15)
    if not direct:
        means = means.reshape(15 * PBX, LANES)
        means = jnp.pad(means, ((0, count * share - 15 * PBX), (0, 0)))
        means = means.reshape(count, share, LANES)
    spread = lax.all_to_all(means, "tile", 0, 0, tiled=True)
    advanced = parent_run(wave_speed, parent_state, low, high, metrics)
    returned = lax.all_to_all(reorder(meta, spread), "tile", 0, 0, tiled=True)
    nest_next = nest_out(final)
    if not direct:
        returned = returned.reshape(count * share, LANES)[: 15 * PBX].reshape(15, PBX, LANES)
    parent_next = insert(meta, returned, advanced)
    return (parent_next, nest_next)


def solution(mesh):
    in_specs = (
        P(None, None, ("member", "tile"), None),
        P(("member", "tile"), None, None, None, None),
        P(None, "tile", None),
        P(),
        P(),
    )
    out_specs = (
        P(None, None, ("member", "tile"), None),
        P(("member", "tile"), None, None, None, None),
    )
    return jax.shard_map(body, mesh=mesh, in_specs=in_specs, out_specs=out_specs, check_vma=False)
```

time: 330 us -> 71.8 us (0.22)
  the two profiles are of different devices: /device:TPU:1 before, /device:TPU:0 now
where the time goes in v1:
time: 71.8 us; the launch traced here: 71.3 us
  Pallas kernels  27.4 us (38%)
  starting transfers between devices  15.4 us (21%)
  blocking collectives  14.8 us (21%)
  local copies, waits for them, and re-layouts  12.2 us (17%)
  between operations  0.76 us (1%)
  waiting for transfers between devices  0.72 us (1%)
    all_to_all x1, blocking collectives, body(): spread = lax.all_to_all(means, 'tile', 0, 0, tiled=True)  14.8 us
    unnamed x18, local copies, waits for them, and re-layouts  12.2 us
    pallas_call x1, Pallas kernels, parent_run(): pl.pallas_call(parent_kernel, out_shape=jax.ShapeDtypeStruct(parent_state...  10.9 us
    all_to_all x1, starting transfers between devices, body(): recv = lax.all_to_all(slots, 'tile', 0, 0, tiled=True)  7.4 us
    pallas_call x1, Pallas kernels, nest_run(): pl.pallas_call(nest_kernel, out_shape=(jax.ShapeDtypeStruct(PACKED, F32),...  6.97 us
    ppermute x1, starting transfers between devices, body(): high = lax.ppermute(down, 'tile', backward)  4.08 us
    all_to_all x1, starting transfers between devices, body(): returned = lax.all_to_all(reorder(meta, spread), 'tile', 0, 0, tiled=True)  3.51 us
    pallas_call x1, Pallas kernels, nest_in(): pl.pallas_call(nest_in_kernel, out_shape=jax.ShapeDtypeStruct(PACKED, F32...  2.44 us
  transfers between devices with their start and end apart: 4, of which 1 were waited for; matrix products, arithmetic and copies ran while one was open for 5% of the time, Pallas kernels for 34%

profile of v1, /device:TPU:0, one launch (start us, length us, event | category | flops | bytes accessed | tf_op | source)
XLA Modules:
  0.0 71.3 jit_solution(14780622744887139986)
XLA Ops:
  0.6 1.9 %copy.8.parent_ref = f32[5,8,12,768]{3,2,1,0:T(8,128)S(1)} copy(f32[5,8,12,768]{3,1,2,0:T(8,128)} %param.5) | data formatting | bytes 2949120 | tf_op args[0]
  2.6 2.2 %prepare.1 = (s32[24]{0:T(128)S(1)}, f32[16,24,128]{2,1,0:T(8,128)}, f32[43,4,768]{2,1,0:T(4,128)}, f32[43,4,768]{2,1,0:T(4,128)}) custom-call(s32[16]{0:T(128)S(1)} %copy-done.6, f32[5,8,12,768]{3,2,1,0:T(8,128)S(1)} %copy.8.parent_ref, f32[3,12,768]{2,1,0:T(8,128)S(1)} %copy-done.4), custom_call_target="tpu_custom_call" | custom-call | flops 4000000 | bytes 4000000 | tf_op jit(solution)/shard_map/prepare/pallas_call | solution.py:154
  4.8 7.4 %all-to-all-start = ((f32[16,24,128]{2,1,0:T(8,128)}), f32[16,24,128]{2,1,0:T(8,128)S(1)}, u32[]{:S(2)}, u32[]{:S(2)}) async-start(f32[16,24,128]{2,1,0:T(8,128)} %get-tuple-element.9), calls=%async_computation | async-start | bytes 393216 | tf_op jit(solution)/shard_map/all_to_all | solution.py:621
  12.2 0.4 collective-permute-start
  12.6 4.1 %collective-permute-start.1 = (f32[43,4,768]{2,1,0:T(4,128)}, f32[43,4,768]{2,1,0:T(4,128)}, u32[]{:S(2)}, u32[]{:S(2)}) collective-permute-start(f32[43,4,768]{2,1,0:T(4,128)} %get-tuple-element.12), channel_id=1, source_target_pairs={{1,0},{2,1},{3,2},{4,3},{5,4},{6,5},{7,6},{8,7},{9,8},{10,9},{11,1... | collective-permute-start | bytes 1585160 | tf_op jit(solution)/shard_map/ppermute | solution.py:623
  16.7 1.8 %copy.9.nest_ref = f32[1,5,8,36,144]{4,3,2,1,0:T(8,128)S(1)} copy(f32[1,5,8,36,144]{4,2,3,1,0:T(8,128)} %param.6) | data formatting | bytes 1658880 | tf_op args[1]
  18.6 0.0 copy-start.5
  18.6 2.4 %nest_in.1.start_ref = f32[5,9,5,8,128]{4,3,2,1,0:T(8,128)S(1)} custom-call(f32[1,5,8,36,144]{4,3,2,1,0:T(8,128)S(1)} %copy.9.nest_ref), custom_call_target="tpu_custom_call" | custom-call | flops 8000000 | bytes 6000000 | tf_op jit(solution)/shard_map/nest_in/pallas_call | solution.py:237
  21.0 0.7 all-to-all-done.recv_ref
  21.7 7.0 %nest_run.1 = (f32[5,9,5,8,128]{4,3,2,1,0:T(8,128)S(1)}, f32[16,12,128]{2,1,0:T(8,128)S(1)}) custom-call(s32[24]{0:T(128)S(1)} %get-tuple-element.8.meta_ref, f32[8]{0:T(128)S(1)} %copy-done.5, f32[16,24,128]{2,1,0:T(8,128)S(1)} %all-to-all-done.recv_ref, f32[5,9,5,8,128]{4,3,2,1,0:T(8,128)S(1)} %nest_in.1.start_ref), custom_call_target="tpu_custom_call" | custom-call | flops 40000000 | bytes 3000000 | tf_op jit(solution)/shard_map/nest_run/pallas_call | solution.py:431
  28.7 0.0 copy-start.2
  28.7 0.9 %copy-done.2 = f32[5,9,5,8,128]{4,3,2,1,0:T(8,128)} copy-done((f32[5,9,5,8,128]{4,3,2,1,0:T(8,128)}, f32[5,9,5,8,128]{4,3,2,1,0:T(8,128)S(1)}, u32[]{:S(2)}) %copy-start.2) | copy-done | bytes 921624
  29.6 14.8 %all_to_all.15.in_ref = f32[16,12,128]{2,1,0:T(8,128)S(1)} all-to-all(f32[16,12,128]{2,1,0:T(8,128)S(1)} %get-tuple-element.10), channel_id=1, replica_groups=mesh['member'=2,'tile'=16] {'tile'}, dimensions={0} | all-to-all | bytes 196608 | tf_op jit(solution)/shard_map/all_to_all | solution.py:632
  44.4 1.3 %reorder.1 = f32[16,12,128]{2,1,0:T(8,128)} custom-call(s32[24]{0:T(128)S(1)} %get-tuple-element.8.meta_ref, f32[16,12,128]{2,1,0:T(8,128)S(1)} %all_to_all.15.in_ref), custom_call_target="tpu_custom_call" | custom-call | flops 100000 | bytes 200000 | tf_op jit(solution)/shard_map/reorder/pallas_call | solution.py:537
  45.7 3.5 %all-to-all-start.2 = ((f32[16,12,128]{2,1,0:T(8,128)}), f32[16,12,128]{2,1,0:T(8,128)S(1)}, u32[]{:S(2)}, u32[]{:S(2)}) async-start(f32[16,12,128]{2,1,0:T(8,128)} %reorder.1), calls=%async_computation.2 | async-start | bytes 262144 | tf_op jit(solution)/shard_map/all_to_all | solution.py:634
  49.3 0.0 copy-start.3
  49.3 1.2 %copy-done.3 = f32[5,9,5,8,128]{4,3,2,1,0:T(8,128)S(1)} copy-done((f32[5,9,5,8,128]{4,3,2,1,0:T(8,128)S(1)}, f32[5,9,5,8,128]{4,3,2,1,0:T(8,128)}, u32[]{:S(2)}) %copy-start.3) | copy-done | bytes 921624
  50.4 2.3 %nest_out.1 = f32[1,5,8,36,144]{4,3,2,1,0:T(8,128)S(1)} custom-call(f32[5,9,5,8,128]{4,3,2,1,0:T(8,128)S(1)} %copy-done.3), custom_call_target="tpu_custom_call" | custom-call | flops 8000000 | bytes 6000000 | tf_op jit(solution)/shard_map/nest_out/pallas_call | solution.py:275
  52.8 1.6 %copy.12 = f32[1,5,8,36,144]{4,2,3,1,0:T(8,128)} copy(f32[1,5,8,36,144]{4,3,2,1,0:T(8,128)S(1)} %nest_out.1) | data formatting | bytes 1658880
  54.3 10.9 %parent_run.1.parent_ref = f32[5,8,12,768]{3,2,1,0:T(8,128)S(1)} custom-call(f32[8]{0:T(128)S(1)} %copy-done.5, f32[5,8,12,768]{3,2,1,0:T(8,128)S(1)} %copy.8.parent_ref, f32[43,4,768]{2,1,0:T(4,128)} %collective-permute-done.low_ref, f32[43,4,768]{2,1,0:T(4,128)} %collective-permute-done.1.high_ref, f32[3,12,768]{2,1,0:T(8,128)S(1)} %copy-done.4), custom_call_target="tpu_custom_call" | custom-call | flops 40000000 | bytes 8000000 | tf_op jit(solution)/shard_map/parent_run/pallas_call | solution.py:512
  65.3 1.3 %copy-done = f32[5,8,12,768]{3,2,1,0:T(8,128)} copy-done((f32[5,8,12,768]{3,2,1,0:T(8,128)}, f32[5,8,12,768]{3,2,1,0:T(8,128)S(1)}, u32[]{:S(2)}) %copy-start) | copy-done | bytes 1474584
  66.6 1.5 %copy-done.1 = f32[5,8,12,768]{3,2,1,0:T(8,128)S(1)} copy-done((f32[5,8,12,768]{3,2,1,0:T(8,128)S(1)}, f32[5,8,12,768]{3,2,1,0:T(8,128)}, u32[]{:S(2)}) %copy-start.1) | copy-done | bytes 1474584
  68.1 1.2 %insert.1 = f32[5,8,12,768]{3,2,1,0:T(8,128)S(1)} custom-call(s32[24]{0:T(128)S(1)} %get-tuple-element.8.meta_ref, f32[16,12,128]{2,1,0:T(8,128)S(1)} %all-to-all-done.2.mean_ref, f32[5,8,12,768]{3,2,1,0:T(8,128)S(1)} %copy-done.1), custom_call_target="tpu_custom_call", output_to_operand_aliasing={{}: (2, {})} | custom-call | flops 4000000 | bytes 2000000 | tf_op jit(solution)/shard_map/insert/pallas_call | solution.py:596
  69.3 2.0 %copy.11 = f32[5,8,12,768]{3,1,2,0:T(8,128)} copy(f32[5,8,12,768]{3,2,1,0:T(8,128)S(1)} %insert.1) | data formatting | bytes 2949120
  (10 shorter events, 0.0 us)
Async XLA Ops:
  0.6 1.9 %copy-start.4 = (f32[3,12,768]{2,1,0:T(8,128)S(1)}, f32[3,12,768]{2,1,0:T(8,128)}, u32[]{:S(2)}) copy-start(f32[3,12,768]{2,1,0:T(8,128)} %metrics_ref.3) | copy-start | bytes 331780
  0.6 1.9 %copy-start.6 = (s32[16]{0:T(128)S(1)}, s32[16]{0:T(128)}, u32[]{:S(2)}) copy-start(s32[16]{0:T(128)} %patch_ref.1) | copy-start | bytes 196
  4.8 16.9 %all-to-all-start = ((f32[16,24,128]{2,1,0:T(8,128)}), f32[16,24,128]{2,1,0:T(8,128)S(1)}, u32[]{:S(2)}, u32[]{:S(2)}) async-start(f32[16,24,128]{2,1,0:T(8,128)} %get-tuple-element.9), calls=%async_computation | async-start | bytes 393216 | tf_op jit(solution)/shard_map/all_to_all | solution.py:621
  12.2 42.1 %collective-permute-start = (f32[43,4,768]{2,1,0:T(4,128)}, f32[43,4,768]{2,1,0:T(4,128)}, u32[]{:S(2)}, u32[]{:S(2)}) collective-permute-start(f32[43,4,768]{2,1,0:T(4,128)} %get-tuple-element.11), channel_id=1, source_target_pairs={{0,1},{1,2},{2,3},{3,4},{4,5},{5,6},{6,7},{7,8},{8,9},{9,10},{10,1... | collective-permute-start | bytes 1585160 | tf_op jit(solution)/shard_map/ppermute | solution.py:622
  12.6 41.7 %collective-permute-start.1 = (f32[43,4,768]{2,1,0:T(4,128)}, f32[43,4,768]{2,1,0:T(4,128)}, u32[]{:S(2)}, u32[]{:S(2)}) collective-permute-start(f32[43,4,768]{2,1,0:T(4,128)} %get-tuple-element.12), channel_id=1, source_target_pairs={{1,0},{2,1},{3,2},{4,3},{5,4},{6,5},{7,6},{8,7},{9,8},{10,9},{11,1... | collective-permute-start | bytes 1585160 | tf_op jit(solution)/shard_map/ppermute | solution.py:623
  18.6 3.2 %copy-start.5 = (f32[8]{0:T(128)S(1)}, f32[8]{0:T(128)}, u32[]{:S(2)}) copy-start(f32[8]{0:T(128)} %speed_ref.3) | copy-start | bytes 100
  28.7 0.9 %copy-start.2 = (f32[5,9,5,8,128]{4,3,2,1,0:T(8,128)}, f32[5,9,5,8,128]{4,3,2,1,0:T(8,128)S(1)}, u32[]{:S(2)}) copy-start(f32[5,9,5,8,128]{4,3,2,1,0:T(8,128)S(1)} %get-tuple-element.13.packed_ref) | copy-start | bytes 2764804
  45.7 20.8 %all-to-all-start.2 = ((f32[16,12,128]{2,1,0:T(8,128)}), f32[16,12,128]{2,1,0:T(8,128)S(1)}, u32[]{:S(2)}, u32[]{:S(2)}) async-start(f32[16,12,128]{2,1,0:T(8,128)} %reorder.1), calls=%async_computation.2 | async-start | bytes 262144 | tf_op jit(solution)/shard_map/all_to_all | solution.py:634
  49.3 1.2 %copy-start.3 = (f32[5,9,5,8,128]{4,3,2,1,0:T(8,128)S(1)}, f32[5,9,5,8,128]{4,3,2,1,0:T(8,128)}, u32[]{:S(2)}) copy-start(f32[5,9,5,8,128]{4,3,2,1,0:T(8,128)} %copy-done.2) | copy-start | bytes 2764804
  65.3 1.3 %copy-start = (f32[5,8,12,768]{3,2,1,0:T(8,128)}, f32[5,8,12,768]{3,2,1,0:T(8,128)S(1)}, u32[]{:S(2)}) copy-start(f32[5,8,12,768]{3,2,1,0:T(8,128)S(1)} %parent_run.1.parent_ref) | copy-start | bytes 4423684
  66.6 1.5 %copy-start.1 = (f32[5,8,12,768]{3,2,1,0:T(8,128)S(1)}, f32[5,8,12,768]{3,2,1,0:T(8,128)}, u32[]{:S(2)}) copy-start(f32[5,8,12,768]{3,2,1,0:T(8,128)} %copy-done) | copy-start | bytes 4423684

commit v2 on v1

v2 whole, which is shorter than its diff:
```python
import functools

import jax
import jax.numpy as jnp
from jax import lax
from jax.experimental import pallas as pl
from jax.experimental.pallas import tpu as pltpu
from jax.sharding import PartitionSpec as P

PBX = 12
PBY = 48
NSTEP = 4
DIFFUSION = 0.1

FIELDS = 5
LEVELS = 8
FX = 3 * PBX
FY = 3 * PBY
LANES = 128
GROUPS = 16
COLS = FY // GROUPS
ROWS = 5
SLOT = 24
META = 8
F32 = jnp.float32
BF16 = jnp.bfloat16
VMEM = pl.BlockSpec(memory_space=pltpu.VMEM)
SMEM = pl.BlockSpec(memory_space=pltpu.SMEM)
HBM = pl.BlockSpec(memory_space=pltpu.HBM)
TOKEN = jax.ShapeDtypeStruct((8, LANES), F32)


def params(mebibytes=24):
    return pltpu.CompilerParams(vmem_limit_bytes=mebibytes * 1024 * 1024)


def cost(flops, moved):
    return pl.CostEstimate(flops=flops, bytes_accessed=moved, transcendentals=0)


def iota(shape, dim):
    return lax.broadcasted_iota(jnp.int32, shape, dim)


def chooser(mask):
    return jnp.where(mask, 1.0, 0.0).astype(BF16)


def pick(values, matrix, terms):
    total = None
    for term in range(terms):
        part = values.astype(BF16)
        piece = jnp.dot(part, matrix, preferred_element_type=F32)
        total = piece if total is None else total + piece
        if term + 1 < terms:
            values = values - part.astype(F32)
    return total


def level_speeds(speed_ref, index):
    speeds = jnp.zeros(index.shape, F32)
    for level in range(LEVELS):
        speeds = jnp.where(index == level, speed_ref[level], speeds)
    return speeds


def prepare_kernel(
    per_device,
    patch_ref,
    parent_ref,
    metrics_ref,
    meta_ref,
    slots_ref,
    up_ref,
    down_ref,
    strips_ref,
    lines_ref,
    cells_ref,
    sides_ref,
    sems,
):
    count = patch_ref.shape[0]
    rows, columns = parent_ref.shape[1], parent_ref.shape[3]
    me = lax.axis_index("tile")
    copies = []

    def fetch(source, target):
        copy = pltpu.make_async_copy(source, target, sems.at[len(copies)])
        copy.start()
        copies.append(copy)

    def note(block, carry):
        meta_ref[META + patch_ref[block] // per_device] = block
        return carry

    lax.fori_loop(0, count, note, 0)
    own = meta_ref[META + me]
    after = meta_ref[META + lax.rem(me + 1, count)]
    before = meta_ref[META + lax.rem(me + count - 1, count)]
    meta_ref[0] = patch_ref[me] // per_device
    meta_ref[1] = lax.rem(patch_ref[own], per_device) * PBY
    last_window = columns - 2 * LANES

    def place(block):
        first = lax.rem(patch_ref[block], per_device) * PBY
        window = jnp.minimum(first // LANES * LANES, last_window)
        return first, pl.multiple_of(window, LANES)

    def window_matrix(offset):
        source = iota((2 * LANES, LANES), 0)
        lane = iota((2 * LANES, LANES), 1)
        wanted = offset + 3 * lax.rem(lane, GROUPS) + lane // GROUPS
        return chooser((source == wanted) & (lane < PBY))

    first, window = place(own)
    left = lax.rem(first + columns - 1, columns)
    right = lax.rem(first + PBY, columns)
    beside = ((after, rows - 1), (before, 0))
    for side, column in enumerate((left, right)):
        block = pl.multiple_of(column // LANES * LANES, LANES)
        fetch(parent_ref.at[:, :, :, pl.ds(block, LANES)], strips_ref.at[side])
    for side, (block, row) in enumerate(beside):
        fetch(parent_ref.at[:, row, :, pl.ds(place(block)[1], 2 * LANES)], lines_ref.at[side])
    for index, (target_ref, start) in enumerate(((up_ref, rows - NSTEP), (down_ref, 0))):
        for field in range(FIELDS):
            fetch(
                parent_ref.at[field, pl.ds(start, NSTEP)],
                target_ref.at[pl.ds(field * NSTEP, NSTEP)],
            )
        for kind in range(3):
            sides_ref[index, kind // 2, pl.ds(kind % 2 * NSTEP, NSTEP), :] = metrics_ref[
                kind, pl.ds(start, NSTEP), :
            ]
        fetch(sides_ref.at[index], target_ref.at[pl.ds(FIELDS * NSTEP, 2)])

    for kind in range(3):
        cells_ref[pl.ds(kind * 16, PBX), :] = metrics_ref[kind, :, pl.ds(window, 2 * LANES)]
    mets = pick(cells_ref[...], window_matrix(first - window), 3)
    mets = [mets[kind * 16 : kind * 16 + 16] for kind in range(3)]
    lane = iota((16, LANES), 1)
    packed = jnp.where(
        lane < PBY,
        mets[0],
        jnp.where(lane < 2 * PBY, pltpu.roll(mets[1], PBY, 1), pltpu.roll(mets[2], 2 * PBY, 1)),
    )
    last = jnp.where((lane >= 32) & (lane < PBY), mets[2], 0.0)
    for shift in (64, 32, 16):
        last = last + pltpu.roll(last, shift, 1)
    last = jnp.where(lane // GROUPS == lax.rem(iota((16, LANES), 0), 8), last, 0.0)
    slots_ref[own, pl.ds(8, PBX), :] = packed[:PBX]
    slots_ref[own, pl.ds(20, 1), :] = jnp.sum(last[:8], axis=0, keepdims=True)
    slots_ref[own, pl.ds(21, 1), :] = jnp.sum(last[8:12], axis=0, keepdims=True)

    lane = iota((LEVELS, LANES), 1)
    edges = jnp.zeros((LEVELS, LANES), F32)
    for side, column in enumerate((left, right)):
        copies[side].wait()
        same = chooser(iota((LANES, LANES), 0) == lax.rem(column, LANES))
        strips = strips_ref[side].reshape(FIELDS * PBX * LEVELS, LANES)
        strips = pick(strips, same, 3)
        for field in range(FIELDS):
            for row in range(PBX):
                at = (field * PBX + row) * LEVELS
                target = row * 10 + field * 2 + side
                edges = jnp.where(lane == target, strips[at : at + LEVELS], edges)
    slots_ref[own, pl.ds(0, 8), :] = edges

    for side, (block, row) in enumerate(beside):
        first, window = place(block)
        copies[2 + side].wait()
        lines = lines_ref[side].reshape(FIELDS * LEVELS, 2 * LANES)
        found = pick(lines, window_matrix(first - window), 3)
        found = [found[field * LEVELS : (field + 1) * LEVELS] for field in range(FIELDS)]
        for pair in range(2):
            slots_ref[block, pl.ds(8 * pair, 8), :] = jnp.where(
                lane < PBY, found[2 * pair], pltpu.roll(found[2 * pair + 1], PBY, 1)
            )
        slots_ref[block, pl.ds(16, 8), :] = found[4]
    for copy in copies[4:]:
        copy.wait()


def prepare(nest_patch, parent_state, metrics, per_device):
    count = nest_patch.shape[0]
    columns = parent_state.shape[3]
    halo = jax.ShapeDtypeStruct((FIELDS * NSTEP + 2, LEVELS, columns), F32)
    return pl.pallas_call(
        functools.partial(prepare_kernel, per_device),
        out_shape=(
            jax.ShapeDtypeStruct((META + count,), jnp.int32),
            jax.ShapeDtypeStruct((count, SLOT, LANES), F32),
            halo,
            halo,
        ),
        in_specs=[SMEM, HBM, VMEM],
        out_specs=(SMEM, VMEM, VMEM, VMEM),
        scratch_shapes=[
            pltpu.VMEM((2, FIELDS, PBX, LEVELS, LANES), F32),
            pltpu.VMEM((2, FIELDS, LEVELS, 2 * LANES), F32),
            pltpu.VMEM((48, 2 * LANES), F32),
            pltpu.VMEM((2, 2, LEVELS, columns), F32),
            pltpu.SemaphoreType.DMA((4 + 2 * FIELDS + 2,)),
        ],
        compiler_params=params(60),
        cost_estimate=cost(4_000_000, 4_000_000),
        name="prepare",
    )(nest_patch, parent_state, metrics)


def swap_chunks(parts):
    chunk = iota((8, LANES), 1) // GROUPS
    parts = list(parts)
    for bit in (1, 2, 4):
        high = (chunk & bit) != 0
        for low_index in range(8):
            if low_index & bit:
                continue
            high_index = low_index | bit
            low_part, high_part = parts[low_index], parts[high_index]
            parts[low_index] = jnp.where(high, pltpu.roll(high_part, GROUPS * bit, 1), low_part)
            parts[high_index] = jnp.where(
                high, high_part, pltpu.roll(low_part, LANES - GROUPS * bit, 1)
            )
    return parts


def column_order(shape, natural_dim):
    natural = iota(shape, natural_dim)
    packed = iota(shape, 1 - natural_dim)
    return chooser(
        (natural == COLS * lax.rem(packed, GROUPS) + packed // GROUPS) & (packed < FY)
    )


def nest_in_kernel(nest_ref, out_ref):
    order = column_order((FY, 2 * LANES), 0)

    def one_field(field, carry):
        plain = nest_ref[0, field].reshape(FX * LEVELS, FY)
        mixed = pick(plain, order, 2)
        for row in range(ROWS):
            parts, extra = [], None
            for group in range(8):
                at = (ROWS * group + row) * LEVELS
                if at >= FX * LEVELS:
                    parts.append(jnp.zeros((LEVELS, LANES), F32))
                    continue
                parts.append(mixed[at : at + LEVELS, :LANES])
                piece = mixed[at : at + LEVELS, LANES:]
                extra = extra + pltpu.roll(piece, GROUPS * group, 1) if group else piece
            parts = swap_chunks(parts) + [extra]
            for col in range(COLS):
                out_ref[field, col, row] = parts[col]
        return carry

    lax.fori_loop(0, FIELDS, one_field, 0)


PACKED = (FIELDS, COLS, ROWS, 8, LANES)


def nest_in(nest_state):
    return pl.pallas_call(
        nest_in_kernel,
        out_shape=jax.ShapeDtypeStruct(PACKED, F32),
        in_specs=[VMEM],
        out_specs=VMEM,
        compiler_params=params(),
        cost_estimate=cost(8_000_000, 6_000_000),
        name="nest_in",
    )(nest_state)


def nest_out_kernel(packed_ref, after_ref, out_ref, token_ref, mixed_ref):
    order = column_order((2 * LANES, FY), 1)
    few = iota((8, LANES), 1) < GROUPS

    def one_field(field, carry):
        for row in range(ROWS):
            parts = swap_chunks([packed_ref[field, col, row] for col in range(8)])
            extra = packed_ref[field, 8, row]
            for group in range(8):
                fine = ROWS * group + row
                if fine >= FX:
                    continue
                turned = pltpu.roll(extra, LANES - GROUPS * group, 1) if group else extra
                mixed_ref[pl.ds(fine * LEVELS, LEVELS), pl.ds(0, LANES)] = parts[group]
                mixed_ref[pl.ds(fine * LEVELS, LEVELS), pl.ds(LANES, LANES)] = jnp.where(
                    few, turned, 0.0
                )
        out_ref[0, field] = pick(mixed_ref[...], order, 2).reshape(FX, LEVELS, FY)
        return carry

    lax.fori_loop(0, FIELDS, one_field, 0)

def nest_out(packed, after):
    return pl.pallas_call(
        nest_out_kernel,
        out_shape=(jax.ShapeDtypeStruct((1, FIELDS, FX, LEVELS, FY), F32), TOKEN),
        in_specs=[VMEM, HBM],
        out_specs=(VMEM, HBM),
        scratch_shapes=[pltpu.VMEM((FX * LEVELS, 2 * LANES), F32)],
        compiler_params=params(),
        cost_estimate=cost(8_000_000, 6_000_000),
        name="nest_out",
    )(packed, after)


def substep(centre, east, west, north, south, coef, speeds):
    by_area, by_x, by_y, half_x, half_y = coef
    spread = [
        (1.0 - 4.0 * DIFFUSION) * centre[f]
        + DIFFUSION * ((east[f] + west[f]) + (north[f] + south[f]))
        for f in range(FIELDS)
    ]
    height = spread[0] - by_area * ((centre[1] - west[1]) + (centre[2] - south[2]))
    zonal = spread[1] - by_x * (east[0] - centre[0])
    merid = spread[2] - by_y * (north[0] - centre[0])
    theta = spread[3] - (
        centre[1] * (east[3] - west[3]) * half_x + centre[2] * (north[3] - south[3]) * half_y
    )
    vertical = spread[4] + speeds * (centre[3] - centre[0])
    return height, zonal, merid, theta, vertical


def nest_kernel(
    meta_ref,
    speed_ref,
    recv_ref,
    start_ref,
    out_ref,
    mean_ref,
    token_ref,
    a_ref,
    b_ref,
    coef_ref,
    rim_ref,
):
    count = recv_ref.shape[0]
    host = meta_ref[0]
    lane = iota((8, LANES), 1)
    chunk = lane // GROUPS
    group = lax.rem(lane, GROUPS)
    sub = iota((8, LANES), 0)
    spare = lane >= LANES - GROUPS
    speeds = level_speeds(speed_ref, sub)

    source = recv_ref[host]
    last = [jnp.where(chunk == sub, source[20 + k : 21 + k], 0.0) for k in range(2)]
    for shift in (64, 32, 16):
        last = [piece + pltpu.roll(piece, shift, 1) for piece in last]
    last = jnp.concatenate(last, axis=0)[:PBX]
    fine = iota((64, PBX), 0)
    coarse_row = jnp.minimum((ROWS * (fine // 8) + lax.rem(fine, 8)) // 3, PBX - 1)
    rows = chooser(coarse_row == iota((64, PBX), 1))
    both = jnp.concatenate([source[8:20], last], axis=1)
    expanded = None
    for term in range(3):
        part = both.astype(BF16)
        piece = jnp.dot(rows, part, preferred_element_type=F32)
        expanded = piece if expanded is None else expanded + piece
        both = both - part.astype(F32)
    kinds = swap_chunks([expanded[8 * k : 8 * k + 8, :LANES] for k in range(8)])
    extra = expanded[:8, LANES:]
    for k in range(1, 8):
        extra = jnp.where(chunk == k, expanded[8 * k : 8 * k + 8, LANES:], extra)
    kinds.append(extra)
    for row in range(ROWS):
        for index in range(9):
            piece = kinds[index][row : row + 1] * speeds
            kind, third = index // 3, index % 3
            if kind == 2:
                coef_ref[third, row, 0] = piece
            else:
                coef_ref[third, row, 1 + kind] = piece
                coef_ref[third, row, 3 + kind] = 0.5 * piece
    edges = source[:8]
    for row in range(ROWS):
        mixed = jnp.zeros((8, LANES), F32)
        for k in range(8):
            coarse = min((ROWS * k + row) // 3, PBX - 1)
            shift = (GROUPS * k - 10 * coarse) % LANES
            turned = pltpu.roll(edges, shift, 1) if shift else edges
            mixed = jnp.where(chunk == k, turned, mixed)
        for field in range(FIELDS):
            lefts = pltpu.roll(mixed, LANES - 2 * field, 1) if field else mixed
            rim_ref[field, row] = jnp.where(
                group == 0, lefts, pltpu.roll(mixed, 14 - 2 * field, 1)
            )

    def line_of(slot, index):
        field, third = index // 3, index % 3
        values = recv_ref[slot, pl.ds(field // 2 * 8, 8), :]
        shift = (LANES - GROUPS - PBY * (field % 2) - GROUPS * third) % LANES
        return pltpu.roll(values, shift, 1) if shift else values

    above_slot = lax.rem(host + count - 1, count)
    below_slot = lax.rem(host + 1, count)

    def put(ref, field, col, row, value):
        ref[field, col, row] = value
        if col == COLS:
            ref[field, 0, row] = jnp.where(group == 0, rim_ref[field, row], pltpu.roll(value, 1, 1))
        if col == 1:
            ref[field, COLS + 1, row] = jnp.where(
                group == GROUPS - 1, rim_ref[field, row], pltpu.roll(value, LANES - 1, 1)
            )
        if row == ROWS - 1:
            ref[field, col, ROWS] = pltpu.roll(value, GROUPS, 1)
        if row == 0:
            ref[field, col, ROWS + 1] = pltpu.roll(value, LANES - GROUPS, 1)

    for field in range(FIELDS):
        for col in range(COLS):
            if col % 3 == 0:
                top = line_of(above_slot, field * 3 + col // 3)
                bottom = line_of(below_slot, field * 3 + col // 3)
            for row in range(ROWS):
                value = start_ref[field, col, row]
                if row == 1:
                    value = jnp.where(spare, bottom, value)
                if row == 4:
                    value = jnp.where(spare, top, value)
                put(a_ref, field, col + 1, row, value)

    def one_step(src, dst):
        for col in range(1, COLS + 1):
            third = (col - 1) // 3
            centre = [[src[f, col, row] for f in range(FIELDS)] for row in range(ROWS)]
            for row in range(ROWS):
                east = (
                    centre[row + 1]
                    if row + 1 < ROWS
                    else [src[f, col, ROWS + 1] for f in range(FIELDS)]
                )
                west = centre[row - 1] if row else [src[f, col, ROWS] for f in range(FIELDS)]
                north = [src[f, col + 1, row] for f in range(FIELDS)]
                south = [src[f, col - 1, row] for f in range(FIELDS)]
                coef = [coef_ref[third, row, k] for k in range(5)]
                new = substep(centre[row], east, west, north, south, coef, speeds)
                for f in range(FIELDS):
                    value = new[f]
                    if row in (1, 4):
                        value = jnp.where(spare, centre[row][f], value)
                    put(dst, f, col, row, value)

    def two_steps(index, carry):
        one_step(a_ref, b_ref)
        one_step(b_ref, a_ref)
        return carry

    lax.fori_loop(0, 3 * NSTEP // 2, two_steps, 0)

    for field in range(FIELDS):
        for third in range(3):
            sums = []
            for row in range(ROWS):
                values = [a_ref[field, third * 3 + k + 1, row] for k in range(3)]
                for k in range(3):
                    out_ref[field, third * 3 + k, row] = values[k]
                sums.append(values[0] + values[1] + values[2])
            later = sums + [pltpu.roll(sums[row], LANES - GROUPS, 1) for row in range(2)]
            totals = [
                (later[row] + later[row + 1] + later[row + 2]) * (1.0 / 9.0) for row in range(ROWS)
            ]
            for half in range(2):
                mean = None
                for coarse in range(8 * half, min(8 * half + 8, PBX)):
                    at, row = 3 * coarse // ROWS, 3 * coarse % ROWS
                    shift = GROUPS * (coarse - 8 * half - at) % LANES
                    piece = pltpu.roll(totals[row], shift, 1) if shift else totals[row]
                    mean = piece if mean is None else jnp.where(chunk == coarse % 8, piece, mean)
                mean_ref[field * 3 + third, pl.ds(8 * half, 8), :] = mean

def nest_run(meta, wave_speed, recv, start, pieces):
    padded = (FIELDS, COLS + 2, ROWS + 2, 8, LANES)
    return pl.pallas_call(
        nest_kernel,
        out_shape=(
            jax.ShapeDtypeStruct(PACKED, F32),
            jax.ShapeDtypeStruct((pieces, 16, LANES), F32),
            TOKEN,
        ),
        in_specs=[SMEM, SMEM, VMEM, VMEM],
        out_specs=(VMEM, VMEM, HBM),
        scratch_shapes=[
            pltpu.VMEM(padded, F32),
            pltpu.VMEM(padded, F32),
            pltpu.VMEM((3, ROWS, 5, 8, LANES), F32),
            pltpu.VMEM((FIELDS, ROWS, 8, LANES), F32),
        ],
        compiler_params=params(),
        cost_estimate=cost(40_000_000, 3_000_000),
        name="nest_run",
    )(meta, wave_speed, recv, start)


def parent_kernel(
    speed_ref,
    parent_ref,
    low_ref,
    high_ref,
    metrics_ref,
    after_ref,
    out_ref,
    token_ref,
    a_ref,
    b_ref,
    wide_ref,
    coef_ref,
):
    rows, columns = parent_ref.shape[1], parent_ref.shape[3]
    parts = columns // LANES
    lane = iota((LEVELS, LANES), 1)
    speeds = level_speeds(speed_ref, iota((LEVELS, LANES), 0))
    for field in range(FIELDS):
        for row in range(NSTEP):
            a_ref[field, row] = low_ref[field * NSTEP + row]
            a_ref[field, NSTEP + rows + row] = high_ref[field * NSTEP + row]
        for row in range(rows):
            a_ref[field, NSTEP + row] = parent_ref[field, row]
    for kind in range(3):
        span = pl.ds(kind % 2 * NSTEP, NSTEP)
        wide_ref[kind, pl.ds(0, NSTEP), :] = low_ref[FIELDS * NSTEP + kind // 2, span, :]
        wide_ref[kind, pl.ds(NSTEP, rows), :] = metrics_ref[kind]
        wide_ref[kind, pl.ds(NSTEP + rows, NSTEP), :] = high_ref[FIELDS * NSTEP + kind // 2, span, :]

    for row in range(1, rows + 2 * NSTEP - 1):
        for kind in range(3):
            for part in range(parts):
                span = pl.ds(part * LANES, LANES)
                coef_ref[kind, row, :, span] = wide_ref[kind, pl.ds(row, 1), span] * speeds

    def one_step(src, dst, first, last, moved):
        def one_row(row):
            def block(field, at, part):
                return src[field, at, :, pl.ds(part % parts * LANES, LANES)]

            for part in range(parts):
                centre = [block(f, row, part) for f in range(FIELDS)]
                east = [block(f, row + 1, part) for f in range(FIELDS)]
                west = [block(f, row - 1, part) for f in range(FIELDS)]
                north = [
                    pltpu.roll(
                        jnp.where(lane == 0, block(f, row, part + 1), centre[f]), LANES - 1, 1
                    )
                    for f in range(FIELDS)
                ]
                south = [
                    pltpu.roll(
                        jnp.where(lane == LANES - 1, block(f, row, part + parts - 1), centre[f]), 1, 1
                    )
                    for f in range(FIELDS)
                ]
                span = pl.ds(part * LANES, LANES)
                by_x, by_y, by_area = [coef_ref[kind, row, :, span] for kind in range(3)]
                coef = (by_area, by_x, by_y, 0.5 * by_x, 0.5 * by_y)
                new = substep(centre, east, west, north, south, coef, speeds)
                for f in range(FIELDS):
                    dst[f, row - moved, :, span] = new[f]

        for row in range(first, last):
            one_row(row)

    refs = (a_ref, b_ref)
    for step in range(NSTEP):
        final = step + 1 == NSTEP
        one_step(
            refs[step % 2],
            out_ref if final else refs[(step + 1) % 2],
            step + 1,
            rows + 2 * NSTEP - 1 - step,
            NSTEP if final else 0,
        )


def parent_run(wave_speed, parent_state, low, high, metrics, after):
    rows, columns = parent_state.shape[1], parent_state.shape[3]
    wide = (FIELDS, rows + 2 * NSTEP, LEVELS, columns)
    return pl.pallas_call(
        parent_kernel,
        out_shape=(jax.ShapeDtypeStruct(parent_state.shape, F32), TOKEN),
        in_specs=[SMEM, VMEM, VMEM, VMEM, VMEM, HBM],
        out_specs=(VMEM, HBM),
        scratch_shapes=[
            pltpu.VMEM(wide, F32),
            pltpu.VMEM(wide, F32),
            pltpu.VMEM((3, rows + 2 * NSTEP + 4, columns), F32),
            pltpu.VMEM((3, rows + 2 * NSTEP, LEVELS, columns), F32),
        ],
        compiler_params=params(),
        cost_estimate=cost(40_000_000, 8_000_000),
        name="parent_run",
    )(wave_speed, parent_state, low, high, metrics, after)


def reorder_kernel(meta_ref, in_ref, after_ref, out_ref, token_ref):
    def one(index, carry):
        out_ref[index] = in_ref[meta_ref[META + index]]
        return carry

    lax.fori_loop(0, in_ref.shape[0], one, 0)


def reorder(meta, pieces, after):
    return pl.pallas_call(
        reorder_kernel,
        out_shape=(jax.ShapeDtypeStruct(pieces.shape, F32), TOKEN),
        in_specs=[SMEM, VMEM, HBM],
        out_specs=(VMEM, HBM),
        compiler_params=params(),
        cost_estimate=cost(100_000, 200_000),
        name="reorder",
    )(meta, pieces, after)


def insert_kernel(meta_ref, mean_ref, parent_ref, after_ref, out_ref, rows_ref, window_ref, sem):
    columns = out_ref.shape[3]
    first = meta_ref[1]
    window = pl.multiple_of(jnp.minimum(first // LANES * LANES, columns - 2 * LANES), LANES)
    fetch = pltpu.make_async_copy(
        parent_ref.at[:, :, :, pl.ds(window, 2 * LANES)], window_ref, sem
    )
    fetch.start()
    offset = first - window
    lane = iota((LEVELS, LANES), 1)
    for field in range(FIELDS):
        for row in range(PBX):
            turned = []
            for third in range(3):
                piece = mean_ref[field * 3 + third, pl.ds(row // 8 * 8, 8), :]
                shift = GROUPS * (third - row % 8) % LANES
                turned.append(pltpu.roll(piece, shift, 1) if shift else piece)
            rows_ref[field * PBX + row] = jnp.where(
                lane < GROUPS,
                turned[0],
                jnp.where(lane < 2 * GROUPS, turned[1], jnp.where(lane < PBY, turned[2], 0.0)),
            )
    source = iota((LANES, 2 * LANES), 0)
    target = iota((LANES, 2 * LANES), 1)
    order = chooser(
        (target == offset + 3 * lax.rem(source, GROUPS) + source // GROUPS) & (source < PBY)
    )
    found = pick(rows_ref[...].reshape(FIELDS * PBX * LEVELS, LANES), order, 2)
    found = found.reshape(FIELDS, PBX, LEVELS, 2 * LANES)
    wide = iota((LEVELS, 2 * LANES), 1)
    inside = (wide >= offset) & (wide < offset + PBY)
    fetch.wait()
    for field in range(FIELDS):
        for row in range(PBX):
            window_ref[field, row] = jnp.where(inside, found[field, row], window_ref[field, row])
    store = pltpu.make_async_copy(window_ref, out_ref.at[:, :, :, pl.ds(window, 2 * LANES)], sem)
    store.start()
    store.wait()


def insert(meta, means, advanced, after):
    return pl.pallas_call(
        insert_kernel,
        out_shape=jax.ShapeDtypeStruct(advanced.shape, F32),
        in_specs=[SMEM, VMEM, HBM, HBM],
        out_specs=HBM,
        scratch_shapes=[
            pltpu.VMEM((FIELDS * PBX, LEVELS, LANES), F32),
            pltpu.VMEM((FIELDS, PBX, LEVELS, 2 * LANES), F32),
            pltpu.SemaphoreType.DMA,
        ],
        input_output_aliases={2: 0},
        compiler_params=params(),
        cost_estimate=cost(4_000_000, 2_000_000),
        name="insert",
    )(meta, means, advanced, after)


def body(parent_state, nest_state, metrics, wave_speed, nest_patch):
    count = lax.axis_size("tile")
    rows, columns = parent_state.shape[2:]
    per_device = rows // PBX * (columns // PBY)
    forward = [(i, (i + 1) % count) for i in range(count)]
    backward = [(target, source) for source, target in forward]
    parent_state = jnp.transpose(parent_state, (0, 2, 1, 3))
    nest_state = jnp.transpose(nest_state, (0, 1, 3, 2, 4))

    meta, slots, up, down = prepare(nest_patch, parent_state, metrics, per_device)
    recv = lax.all_to_all(slots, "tile", 0, 0, tiled=True)
    low = lax.ppermute(up, "tile", forward)
    high = lax.ppermute(down, "tile", backward)
    start = nest_in(nest_state)
    direct = 15 <= count < 30
    share = 16 if direct else -(-15 * 16 // count)
    final, means, nested = nest_run(meta, wave_speed, recv, start, count if direct else 15)
    if not direct:
        means = means.reshape(15 * 16, LANES)
        means = jnp.pad(means, ((0, count * share - 15 * 16), (0, 0)))
        means = means.reshape(count, share, LANES)
    spread = lax.all_to_all(means, "tile", 0, 0, tiled=True)
    advanced, stepped = parent_run(wave_speed, parent_state, low, high, metrics, nested)
    mixed, ordered = reorder(meta, spread, stepped)
    returned = lax.all_to_all(mixed, "tile", 0, 0, tiled=True)
    nest_next, unpacked = nest_out(final, ordered)
    if not direct:
        returned = returned.reshape(count * share, LANES)[: 15 * 16].reshape(15, 16, LANES)
    parent_next = insert(meta, returned, advanced, unpacked)
    return (jnp.transpose(parent_next, (0, 2, 1, 3)), jnp.transpose(nest_next, (0, 1, 3, 2, 4)))


def solution(mesh):
    in_specs = (
        P(None, None, ("member", "tile"), None),
        P(("member", "tile"), None, None, None, None),
        P(None, "tile", None),
        P(),
        P(),
    )
    out_specs = (
        P(None, None, ("member", "tile"), None),
        P(("member", "tile"), None, None, None, None),
    )
    return jax.shard_map(body, mesh=mesh, in_specs=in_specs, out_specs=out_specs, check_vma=False)
```

time: 71.8 us -> 63.7 us (0.89)
  blocking collectives: 14.8 us -> 0 us
  starting transfers between devices: 15.4 us -> 25.1 us
  local copies, waits for them, and re-layouts: 12.2 us -> 2.94 us
  waiting for transfers between devices: 0.72 us -> 5.99 us
  Pallas kernels: 27.4 us -> 28.4 us
    all_to_all x1 -> x0, blocking collectives: 14.8 us -> none  [body(): spread = lax.all_to_all(means, 'tile', 0, 0, tiled=True)]
    all_to_all x1 -> x2, starting transfers between devices: 3.51 us -> 13.2 us  [the longest x1 7.21 us: body(): spread = lax.all_to_all(means, 'tile', 0, 0, tiled=True)]
    unnamed x18 -> x12, local copies, waits for them, and re-layouts: 12.2 us -> 2.94 us
    all_to_all x1 -> x2, waiting for transfers between devices: 0.01 us -> 4.62 us  [the longest x1 4.62 us: body(): returned = lax.all_to_all(mixed, 'tile', 0, 0, tiled=True)]
    pallas_call x3, Pallas kernels: 14.5 us -> 11.7 us  [the longest x1 7.03 us: parent_run(): pl.pallas_call(parent_kernel, out_shape=(jax.ShapeDtypeStruct(parent_stat...]
    pallas_call x1, Pallas kernels: 2.25 us -> 4.49 us  [prepare(): pl.pallas_call(functools.partial(prepare_kernel, per_device), out_shape=(...]
    pallas_call x1, Pallas kernels: 1.2 us -> 2.58 us  [insert(): pl.pallas_call(insert_kernel, out_shape=jax.ShapeDtypeStruct(advanced.sha...]
  transfers between devices with their start and end apart: 4 -> 5, of which waited for: 1 -> 2; matrix products, arithmetic and copies ran while one was open for 5% -> 0% of each run, Pallas kernels for 34% -> 32%
where the time goes in v2:
time: 63.7 us; the launch traced here: 63.2 us
  Pallas kernels  28.4 us (45%)
  starting transfers between devices  25.1 us (39%)
  waiting for transfers between devices  5.99 us (9%)
  local copies, waits for them, and re-layouts  2.94 us (5%)
  between operations  0.73 us (1%)
    pallas_call x1, Pallas kernels, nest_run(): pl.pallas_call(nest_kernel, out_shape=(jax.ShapeDtypeStruct(PACKED, F32),...  7.42 us
    all_to_all x1, starting transfers between devices, body(): recv = lax.all_to_all(slots, 'tile', 0, 0, tiled=True)  7.4 us
    all_to_all x1, starting transfers between devices, body(): spread = lax.all_to_all(means, 'tile', 0, 0, tiled=True)  7.21 us
    pallas_call x1, Pallas kernels, parent_run(): pl.pallas_call(parent_kernel, out_shape=(jax.ShapeDtypeStruct(parent_stat...  7.03 us
    all_to_all x1, starting transfers between devices, body(): returned = lax.all_to_all(mixed, 'tile', 0, 0, tiled=True)  6.01 us
    all_to_all x1, waiting for transfers between devices, body(): returned = lax.all_to_all(mixed, 'tile', 0, 0, tiled=True)  4.62 us
    pallas_call x1, Pallas kernels, prepare(): pl.pallas_call(functools.partial(prepare_kernel, per_device), out_shape=(...  4.49 us
    ppermute x1, starting transfers between devices, body(): high = lax.ppermute(down, 'tile', backward)  4.08 us
  transfers between devices with their start and end apart: 5, of which 2 were waited for; matrix products, arithmetic and copies ran while one was open for 0% of the time, Pallas kernels for 32%

profile of v2, /device:TPU:0, one launch (start us, length us, event | category | flops | bytes accessed | tf_op | source)
XLA Modules:
  0.0 63.2 jit_solution(405862940087796013)
XLA Ops:
  0.6 4.5 %prepare.1 = (s32[24]{0:T(128)}, f32[16,24,128]{2,1,0:T(8,128)}, f32[22,8,768]{2,1,0:T(8,128)}, f32[22,8,768]{2,1,0:T(8,128)}) custom-call(s32[16]{0:T(128)} %patch_ref.1, f32[5,12,8,768]{3,2,1,0:T(8,128)} %bitcast.4, f32[3,12,768]{2,1,0:T(8,128)} %metrics_ref.3), custom_call_target="tpu_custom_call" | custom-call | flops 4000000 | bytes 4000000 | tf_op jit(solution)/shard_map/prepare/pallas_call | solution.py:187
  5.1 0.0 copy-start.4
  5.1 0.0 copy-start.5
  5.1 7.4 %all-to-all-start = ((f32[16,24,128]{2,1,0:T(8,128)}), f32[16,24,128]{2,1,0:T(8,128)S(1)}, u32[]{:S(2)}, u32[]{:S(2)}) async-start(f32[16,24,128]{2,1,0:T(8,128)} %get-tuple-element.16), calls=%async_computation | async-start | bytes 393216 | tf_op jit(solution)/shard_map/all_to_all | solution.py:685
  12.6 0.4 collective-permute-start
  13.0 4.1 %collective-permute-start.1 = (f32[22,8,768]{2,1,0:T(8,128)}, f32[22,8,768]{2,1,0:T(8,128)}, u32[]{:S(2)}, u32[]{:S(2)}) collective-permute-start(f32[22,8,768]{2,1,0:T(8,128)} %get-tuple-element.19), channel_id=1, source_target_pairs={{1,0},{2,1},{3,2},{4,3},{5,4},{6,5},{7,6},{8,7},{9,8},{10,9},{11,1... | collective-permute-start | bytes 1622024 | tf_op jit(solution)/shard_map/ppermute | solution.py:687
  17.1 1.4 %copy-done.1 = f32[1,5,8,36,144]{4,2,3,1,0:T(8,128)S(1)} copy-done((f32[1,5,8,36,144]{4,2,3,1,0:T(8,128)S(1)}, f32[1,5,8,36,144]{4,2,3,1,0:T(8,128)}, u32[]{:S(2)}) %copy-start.1) | copy-done | bytes 829464
  18.4 2.3 %nest_in.1.start_ref = f32[5,9,5,8,128]{4,3,2,1,0:T(8,128)S(1)} custom-call(f32[1,5,36,8,144]{4,3,2,1,0:T(8,128)S(1)} %bitcast.6), custom_call_target="tpu_custom_call" | custom-call | flops 8000000 | bytes 6000000 | tf_op jit(solution)/shard_map/nest_in/pallas_call | solution.py:263
  20.7 1.4 %all-to-all-done.recv_ref = f32[16,24,128]{2,1,0:T(8,128)S(1)} async-done(((f32[16,24,128]{2,1,0:T(8,128)}), f32[16,24,128]{2,1,0:T(8,128)S(1)}, u32[]{:S(2)}, u32[]{:S(2)}) %all-to-all-start) | async-done | bytes 196640 | tf_op jit(solution)/shard_map/all_to_all | solution.py:685
  22.1 0.0 copy-done.4
  22.1 7.4 %nest_run.1 = (f32[5,9,5,8,128]{4,3,2,1,0:T(8,128)S(1)}, f32[16,16,128]{2,1,0:T(8,128)S(1)}, f32[8,128]{1,0:T(8,128)S(1)}) custom-call(s32[24]{0:T(128)S(1)} %copy-done.4, f32[8]{0:T(128)S(1)} %copy-done.5, f32[16,24,128]{2,1,0:T(8,128)S(1)} %all-to-all-done.recv_ref, f32[5,9,5,8,128]{4,3,2,1,0:T(8,128)S(1)} %nest_in.1.start_ref), custom_call_target="tpu_custom_call" | custom-call | flops 40000000 | bytes 3000000 | tf_op jit(solution)/shard_map/nest_run/pallas_call | solution.py:477
  29.5 0.6 %copy-done.3 = f32[16,16,128]{2,1,0:T(8,128)} copy-done((f32[16,16,128]{2,1,0:T(8,128)}, f32[16,16,128]{2,1,0:T(8,128)S(1)}, u32[]{:S(2)}) %copy-start.3) | copy-done | bytes 131096
  30.1 7.2 %all-to-all-start.1 = ((f32[16,16,128]{2,1,0:T(8,128)}), f32[16,16,128]{2,1,0:T(8,128)S(1)}, u32[]{:S(2)}, u32[]{:S(2)}) async-start(f32[16,16,128]{2,1,0:T(8,128)} %copy-done.3), calls=%async_computation.1 | async-start | bytes 262144 | tf_op jit(solution)/shard_map/all_to_all | solution.py:696
  37.4 0.0 collective-permute-done.low_ref
  37.4 0.0 collective-permute-done.1.high_ref
  37.4 0.0 copy-start.2
  37.4 0.9 %copy-done.2 = f32[3,12,768]{2,1,0:T(8,128)S(1)} copy-done((f32[3,12,768]{2,1,0:T(8,128)S(1)}, f32[3,12,768]{2,1,0:T(8,128)}, u32[]{:S(2)}) %copy-start.2) | copy-done | bytes 110616
  38.3 7.0 %parent_run.1 = (f32[5,12,8,768]{3,2,1,0:T(8,128)}, f32[8,128]{1,0:T(8,128)S(1)}) custom-call(f32[8]{0:T(128)S(1)} %copy-done.5, f32[5,12,8,768]{3,2,1,0:T(8,128)S(1)} %bitcast.5, f32[22,8,768]{2,1,0:T(8,128)} %collective-permute-done.low_ref, f32[22,8,768]{2,1,0:T(8,128)} %collective-permute-done.1.high_ref, f32[3,12,768]{2,1,0:T(8,128)S(1)} %copy-done.2, ...), custom_call_target="tpu_custom_call" | custom-call | flops 40000000 | bytes 8000000 | tf_op jit(solution)/shard_map/parent_run/pallas_call | solution.py:580
  45.3 0.0 all-to-all-done.1.in_ref
  45.3 1.3 %reorder.1 = (f32[16,16,128]{2,1,0:T(8,128)}, f32[8,128]{1,0:T(8,128)S(1)}) custom-call(s32[24]{0:T(128)S(1)} %copy-done.4, f32[16,16,128]{2,1,0:T(8,128)S(1)} %all-to-all-done.1.in_ref, f32[8,128]{1,0:T(8,128)S(1)} %get-tuple-element.21.after_ref), custom_call_target="tpu_custom_call" | custom-call | flops 100000 | bytes 200000 | tf_op jit(solution)/shard_map/reorder/pallas_call | solution.py:606
  46.6 6.0 %all-to-all-start.2 = ((f32[16,16,128]{2,1,0:T(8,128)}), f32[16,16,128]{2,1,0:T(8,128)S(1)}, u32[]{:S(2)}, u32[]{:S(2)}) async-start(f32[16,16,128]{2,1,0:T(8,128)} %get-tuple-element.22), calls=%async_computation.2 | async-start | bytes 262144 | tf_op jit(solution)/shard_map/all_to_all | solution.py:699
  52.7 3.3 %nest_out.1 = (f32[1,5,36,8,144]{4,3,2,1,0:T(8,128)}, f32[8,128]{1,0:T(8,128)S(1)}) custom-call(f32[5,9,5,8,128]{4,3,2,1,0:T(8,128)S(1)} %get-tuple-element.24.packed_ref, f32[8,128]{1,0:T(8,128)S(1)} %get-tuple-element.25.after_ref), custom_call_target="tpu_custom_call" | custom-call | flops 8000000 | bytes 6000000 | tf_op jit(solution)/shard_map/nest_out/pallas_call | solution.py:297
  56.0 4.6 %all-to-all-done.2.mean_ref = f32[16,16,128]{2,1,0:T(8,128)S(1)} async-done(((f32[16,16,128]{2,1,0:T(8,128)}), f32[16,16,128]{2,1,0:T(8,128)S(1)}, u32[]{:S(2)}, u32[]{:S(2)}) %all-to-all-start.2) | async-done | bytes 131104 | tf_op jit(solution)/shard_map/all_to_all | solution.py:699
  60.6 2.6 %insert.1 = f32[5,12,8,768]{3,2,1,0:T(8,128)} custom-call(s32[24]{0:T(128)S(1)} %copy-done.4, f32[16,16,128]{2,1,0:T(8,128)S(1)} %all-to-all-done.2.mean_ref, f32[5,12,8,768]{3,2,1,0:T(8,128)} %get-tuple-element.23.parent_ref, f32[8,128]{1,0:T(8,128)S(1)} %get-tuple-element.26.after_ref), custom_call_target="tpu_custom_call", output_to_operand_aliasing={{}: (2, {})} | custom-call | flops 4000000 | bytes 2000000 | tf_op jit(solution)/shard_map/insert/pallas_call | solution.py:658
  (5 shorter events, 0.0 us)
Async XLA Ops:
  5.1 16.9 %copy-start.4 = (s32[24]{0:T(128)S(1)}, s32[24]{0:T(128)}, u32[]{:S(2)}) copy-start(s32[24]{0:T(128)} %get-tuple-element.15.meta_ref) | copy-start | bytes 292
  5.1 16.9 %copy-start.5 = (f32[8]{0:T(128)S(1)}, f32[8]{0:T(128)}, u32[]{:S(2)}) copy-start(f32[8]{0:T(128)} %speed_ref.3) | copy-start | bytes 100
  5.1 16.9 %all-to-all-start = ((f32[16,24,128]{2,1,0:T(8,128)}), f32[16,24,128]{2,1,0:T(8,128)S(1)}, u32[]{:S(2)}, u32[]{:S(2)}) async-start(f32[16,24,128]{2,1,0:T(8,128)} %get-tuple-element.16), calls=%async_computation | async-start | bytes 393216 | tf_op jit(solution)/shard_map/all_to_all | solution.py:685
  12.6 24.8 %collective-permute-start = (f32[22,8,768]{2,1,0:T(8,128)}, f32[22,8,768]{2,1,0:T(8,128)}, u32[]{:S(2)}, u32[]{:S(2)}) collective-permute-start(f32[22,8,768]{2,1,0:T(8,128)} %get-tuple-element.18), channel_id=1, source_target_pairs={{0,1},{1,2},{2,3},{3,4},{4,5},{5,6},{6,7},{7,8},{8,9},{9,10},{10,1... | collective-permute-start | bytes 1622024 | tf_op jit(solution)/shard_map/ppermute | solution.py:686
  13.0 24.4 %collective-permute-start.1 = (f32[22,8,768]{2,1,0:T(8,128)}, f32[22,8,768]{2,1,0:T(8,128)}, u32[]{:S(2)}, u32[]{:S(2)}) collective-permute-start(f32[22,8,768]{2,1,0:T(8,128)} %get-tuple-element.19), channel_id=1, source_target_pairs={{1,0},{2,1},{3,2},{4,3},{5,4},{6,5},{7,6},{8,7},{9,8},{10,9},{11,1... | collective-permute-start | bytes 1622024 | tf_op jit(solution)/shard_map/ppermute | solution.py:687
  17.1 1.4 %copy-start.1 = (f32[1,5,8,36,144]{4,2,3,1,0:T(8,128)S(1)}, f32[1,5,8,36,144]{4,2,3,1,0:T(8,128)}, u32[]{:S(2)}) copy-start(f32[1,5,8,36,144]{4,2,3,1,0:T(8,128)} %param.6) | copy-start | bytes 2488324
  18.4 19.0 %copy-start = (f32[5,8,12,768]{3,1,2,0:T(8,128)S(1)}, f32[5,8,12,768]{3,1,2,0:T(8,128)}, u32[]{:S(2)}) copy-start(f32[5,8,12,768]{3,1,2,0:T(8,128)} %param.5) | copy-start | bytes 4423684
  29.5 0.7 %copy-start.3 = (f32[16,16,128]{2,1,0:T(8,128)}, f32[16,16,128]{2,1,0:T(8,128)S(1)}, u32[]{:S(2)}) copy-start(f32[16,16,128]{2,1,0:T(8,128)S(1)} %get-tuple-element.17) | copy-start | bytes 393220
  30.1 15.2 %all-to-all-start.1 = ((f32[16,16,128]{2,1,0:T(8,128)}), f32[16,16,128]{2,1,0:T(8,128)S(1)}, u32[]{:S(2)}, u32[]{:S(2)}) async-start(f32[16,16,128]{2,1,0:T(8,128)} %copy-done.3), calls=%async_computation.1 | async-start | bytes 262144 | tf_op jit(solution)/shard_map/all_to_all | solution.py:696
  37.4 0.9 %copy-start.2 = (f32[3,12,768]{2,1,0:T(8,128)S(1)}, f32[3,12,768]{2,1,0:T(8,128)}, u32[]{:S(2)}) copy-start(f32[3,12,768]{2,1,0:T(8,128)} %metrics_ref.3) | copy-start | bytes 331780
  46.6 13.9 %all-to-all-start.2 = ((f32[16,16,128]{2,1,0:T(8,128)}), f32[16,16,128]{2,1,0:T(8,128)S(1)}, u32[]{:S(2)}, u32[]{:S(2)}) async-start(f32[16,16,128]{2,1,0:T(8,128)} %get-tuple-element.22), calls=%async_computation.2 | async-start | bytes 262144 | tf_op jit(solution)/shard_map/all_to_all | solution.py:699

commit v3 on v2

--- a/solution.py
+++ b/solution.py
@@ -71,10 +71,9 @@
     metrics_ref,
     meta_ref,
     slots_ref,
-    up_ref,
-    down_ref,
-    strips_ref,
-    lines_ref,
+    near_ref,
+    far_ref,
+    mine_ref,
     cells_ref,
     sides_ref,
     sems,
@@ -93,6 +92,22 @@
         meta_ref[META + patch_ref[block] // per_device] = block
         return carry
 
+    odd = lax.rem(me, 2)
+    for index, target_ref in enumerate((near_ref, far_ref)):
+        start = (rows - NSTEP) * (1 - odd if index == 0 else odd)
+        for field in range(FIELDS):
+            fetch(
+                parent_ref.at[field, pl.ds(start, NSTEP)],
+                target_ref.at[pl.ds(field * NSTEP, NSTEP)],
+            )
+        for kind in range(3):
+            sides_ref[index, kind // 2, pl.ds(kind % 2 * NSTEP, NSTEP), :] = jnp.where(
+                odd == index,
+                metrics_ref[kind, pl.ds(rows - NSTEP, NSTEP), :],
+                metrics_ref[kind, pl.ds(0, NSTEP), :],
+            )
+        fetch(sides_ref.at[index], target_ref.at[pl.ds(FIELDS * NSTEP, 2)])
+
     lax.fori_loop(0, count, note, 0)
     own = meta_ref[META + me]
     after = meta_ref[META + lax.rem(me + 1, count)]
@@ -116,23 +131,6 @@
     left = lax.rem(first + columns - 1, columns)
     right = lax.rem(first + PBY, columns)
     beside = ((after, rows - 1), (before, 0))
-    for side, column in enumerate((left, right)):
-        block = pl.multiple_of(column // LANES * LANES, LANES)
-        fetch(parent_ref.at[:, :, :, pl.ds(block, LANES)], strips_ref.at[side])
-    for side, (block, row) in enumerate(beside):
-        fetch(parent_ref.at[:, row, :, pl.ds(place(block)[1], 2 * LANES)], lines_ref.at[side])
-    for index, (target_ref, start) in enumerate(((up_ref, rows - NSTEP), (down_ref, 0))):
-        for field in range(FIELDS):
-            fetch(
-                parent_ref.at[field, pl.ds(start, NSTEP)],
-                target_ref.at[pl.ds(field * NSTEP, NSTEP)],
-            )
-        for kind in range(3):
-            sides_ref[index, kind // 2, pl.ds(kind % 2 * NSTEP, NSTEP), :] = metrics_ref[
-                kind, pl.ds(start, NSTEP), :
-            ]
-        fetch(sides_ref.at[index], target_ref.at[pl.ds(FIELDS * NSTEP, 2)])
-
     for kind in range(3):
         cells_ref[pl.ds(kind * 16, PBX), :] = metrics_ref[kind, :, pl.ds(window, 2 * LANES)]
     mets = pick(cells_ref[...], window_matrix(first - window), 3)
@@ -147,36 +145,38 @@
     for shift in (64, 32, 16):
         last = last + pltpu.roll(last, shift, 1)
     last = jnp.where(lane // GROUPS == lax.rem(iota((16, LANES), 0), 8), last, 0.0)
-    slots_ref[own, pl.ds(8, PBX), :] = packed[:PBX]
-    slots_ref[own, pl.ds(20, 1), :] = jnp.sum(last[:8], axis=0, keepdims=True)
-    slots_ref[own, pl.ds(21, 1), :] = jnp.sum(last[8:12], axis=0, keepdims=True)
+    mine_ref[0, pl.ds(8, PBX), :] = packed[:PBX]
+    mine_ref[0, pl.ds(20, 1), :] = jnp.sum(last[:8], axis=0, keepdims=True)
+    mine_ref[0, pl.ds(21, 1), :] = jnp.sum(last[8:12], axis=0, keepdims=True)
 
     lane = iota((LEVELS, LANES), 1)
     edges = jnp.zeros((LEVELS, LANES), F32)
     for side, column in enumerate((left, right)):
-        copies[side].wait()
+        block = pl.multiple_of(column // LANES * LANES, LANES)
         same = chooser(iota((LANES, LANES), 0) == lax.rem(column, LANES))
-        strips = strips_ref[side].reshape(FIELDS * PBX * LEVELS, LANES)
+        strips = parent_ref[:, :, :, pl.ds(block, LANES)].reshape(FIELDS * PBX * LEVELS, LANES)
         strips = pick(strips, same, 3)
         for field in range(FIELDS):
             for row in range(PBX):
                 at = (field * PBX + row) * LEVELS
                 target = row * 10 + field * 2 + side
                 edges = jnp.where(lane == target, strips[at : at + LEVELS], edges)
-    slots_ref[own, pl.ds(0, 8), :] = edges
+    mine_ref[0, pl.ds(0, 8), :] = edges
+    fetch(mine_ref.at[0], slots_ref.at[own])
 
     for side, (block, row) in enumerate(beside):
         first, window = place(block)
-        copies[2 + side].wait()
-        lines = lines_ref[side].reshape(FIELDS * LEVELS, 2 * LANES)
+        lines = parent_ref[:, row, :, pl.ds(window, 2 * LANES)]
+        lines = lines.reshape(FIELDS * LEVELS, 2 * LANES)
         found = pick(lines, window_matrix(first - window), 3)
         found = [found[field * LEVELS : (field + 1) * LEVELS] for field in range(FIELDS)]
         for pair in range(2):
-            slots_ref[block, pl.ds(8 * pair, 8), :] = jnp.where(
+            mine_ref[1 + side, pl.ds(8 * pair, 8), :] = jnp.where(
                 lane < PBY, found[2 * pair], pltpu.roll(found[2 * pair + 1], PBY, 1)
             )
-        slots_ref[block, pl.ds(16, 8), :] = found[4]
-    for copy in copies[4:]:
+        mine_ref[1 + side, pl.ds(16, 8), :] = found[4]
+        fetch(mine_ref.at[1 + side], slots_ref.at[block])
+    for copy in copies:
         copy.wait()
 
 
@@ -192,14 +192,13 @@
             halo,
             halo,
         ),
-        in_specs=[SMEM, HBM, VMEM],
-        out_specs=(SMEM, VMEM, VMEM, VMEM),
+        in_specs=[SMEM, VMEM, VMEM],
+        out_specs=(SMEM, HBM, HBM, HBM),
         scratch_shapes=[
-            pltpu.VMEM((2, FIELDS, PBX, LEVELS, LANES), F32),
-            pltpu.VMEM((2, FIELDS, LEVELS, 2 * LANES), F32),
+            pltpu.VMEM((3, SLOT, LANES), F32),
             pltpu.VMEM((48, 2 * LANES), F32),
             pltpu.VMEM((2, 2, LEVELS, columns), F32),
-            pltpu.SemaphoreType.DMA((4 + 2 * FIELDS + 2,)),
+            pltpu.SemaphoreType.DMA((3 + 2 * (FIELDS + 1),)),
         ],
         compiler_params=params(60),
         cost_estimate=cost(4_000_000, 4_000_000),
@@ -400,7 +399,9 @@
     def put(ref, field, col, row, value):
         ref[field, col, row] = value
         if col == COLS:
-            ref[field, 0, row] = jnp.where(group == 0, rim_ref[field, row], pltpu.roll(value, 1, 1))
+            ref[field, 0, row] = jnp.where(
+                group == 0, rim_ref[field, row], pltpu.roll(value, 1, 1)
+            )
         if col == 1:
             ref[field, COLS + 1, row] = jnp.where(
                 group == GROUPS - 1, rim_ref[field, row], pltpu.roll(value, LANES - 1, 1)
@@ -424,18 +425,18 @@
                 put(a_ref, field, col + 1, row, value)
 
     def one_step(src, dst):
+        def at(field, col, row):
+            return src[field, col, row]
+
         for col in range(1, COLS + 1):
             third = (col - 1) // 3
-            centre = [[src[f, col, row] for f in range(FIELDS)] for row in range(ROWS)]
+            centre = [[at(f, col, row) for f in range(FIELDS)] for row in range(ROWS)]
             for row in range(ROWS):
-                east = (
-                    centre[row + 1]
-                    if row + 1 < ROWS
-                    else [src[f, col, ROWS + 1] for f in range(FIELDS)]
-                )
-                west = centre[row - 1] if row else [src[f, col, ROWS] for f in range(FIELDS)]
-                north = [src[f, col + 1, row] for f in range(FIELDS)]
-                south = [src[f, col - 1, row] for f in range(FIELDS)]
+                below = row + 1 if row + 1 < ROWS else ROWS + 1
+                east = centre[below] if below < ROWS else [at(f, col, below) for f in range(FIELDS)]
+                west = centre[row - 1] if row else [at(f, col, ROWS) for f in range(FIELDS)]
+                north = [at(f, col + 1, row) for f in range(FIELDS)]
+                south = [at(f, col - 1, row) for f in range(FIELDS)]
                 coef = [coef_ref[third, row, k] for k in range(5)]
                 new = substep(centre[row], east, west, north, south, coef, speeds)
                 for f in range(FIELDS):
@@ -489,49 +490,70 @@
             pltpu.VMEM((3, ROWS, 5, 8, LANES), F32),
             pltpu.VMEM((FIELDS, ROWS, 8, LANES), F32),
         ],
-        compiler_params=params(),
+        compiler_params=params(24),
         cost_estimate=cost(40_000_000, 3_000_000),
         name="nest_run",
     )(meta, wave_speed, recv, start)
 
 
+def patch_window(meta_ref, columns):
+    first = meta_ref[1]
+    return first, pl.multiple_of(jnp.minimum(first // LANES * LANES, columns - 2 * LANES), LANES)
+
+
 def parent_kernel(
+    meta_ref,
     speed_ref,
     parent_ref,
-    low_ref,
-    high_ref,
+    near_ref,
+    far_ref,
     metrics_ref,
     after_ref,
     out_ref,
-    token_ref,
+    window_ref,
     a_ref,
     b_ref,
-    wide_ref,
+    last_ref,
+    sides_ref,
     coef_ref,
+    sems,
 ):
     rows, columns = parent_ref.shape[1], parent_ref.shape[3]
     parts = columns // LANES
+    odd = lax.rem(lax.axis_index("tile"), 2)
+    copies = []
+
+    def move(source, target):
+        copies.append(pltpu.make_async_copy(source, target, sems.at[len(copies)]))
+        copies[-1].start()
+
+    move(parent_ref, a_ref.at[:, pl.ds(NSTEP, rows)])
+    for index, source_ref in enumerate((near_ref, far_ref)):
+        high = 1 - odd if index == 0 else odd
+        for field in range(FIELDS):
+            move(
+                source_ref.at[pl.ds(field * NSTEP, NSTEP)],
+                a_ref.at[field, pl.ds((NSTEP + rows) * high, NSTEP)],
+            )
+        move(source_ref.at[pl.ds(FIELDS * NSTEP, 2)], sides_ref.at[high])
+
     lane = iota((LEVELS, LANES), 1)
     speeds = level_speeds(speed_ref, iota((LEVELS, LANES), 0))
-    for field in range(FIELDS):
-        for row in range(NSTEP):
-            a_ref[field, row] = low_ref[field * NSTEP + row]
-            a_ref[field, NSTEP + rows + row] = high_ref[field * NSTEP + row]
-        for row in range(rows):
-            a_ref[field, NSTEP + row] = parent_ref[field, row]
-    for kind in range(3):
-        span = pl.ds(kind % 2 * NSTEP, NSTEP)
-        wide_ref[kind, pl.ds(0, NSTEP), :] = low_ref[FIELDS * NSTEP + kind // 2, span, :]
-        wide_ref[kind, pl.ds(NSTEP, rows), :] = metrics_ref[kind]
-        wide_ref[kind, pl.ds(NSTEP + rows, NSTEP), :] = high_ref[FIELDS * NSTEP + kind // 2, span, :]
-
-    for row in range(1, rows + 2 * NSTEP - 1):
+
+    def put_coef(row):
         for kind in range(3):
+            if NSTEP <= row < NSTEP + rows:
+                line = metrics_ref[kind, pl.ds(row - NSTEP, 1), :]
+            else:
+                inner = row if row < NSTEP else row - NSTEP - rows
+                line = sides_ref[
+                    int(row >= NSTEP), kind // 2, pl.ds(kind % 2 * NSTEP + inner, 1), :
+                ]
             for part in range(parts):
-                span = pl.ds(part * LANES, LANES)
-                coef_ref[kind, row, :, span] = wide_ref[kind, pl.ds(row, 1), span] * speeds
-
-    def one_step(src, dst, first, last, moved):
+                span = slice(part * LANES, (part + 1) * LANES)
+                coef_ref[kind, row, :, span] = line[:, span] * speeds
+
+    def one_step(src, dst, lines, moved):
         def one_row(row):
             def block(field, at, part):
                 return src[field, at, :, pl.ds(part % parts * LANES, LANES)]
@@ -559,47 +581,69 @@
                 for f in range(FIELDS):
                     dst[f, row - moved, :, span] = new[f]
 
-        for row in range(first, last):
+        for row in lines:
             one_row(row)
 
-    refs = (a_ref, b_ref)
-    for step in range(NSTEP):
-        final = step + 1 == NSTEP
-        one_step(
-            refs[step % 2],
-            out_ref if final else refs[(step + 1) % 2],
-            step + 1,
-            rows + 2 * NSTEP - 1 - step,
-            NSTEP if final else 0,
-        )
-
-
-def parent_run(wave_speed, parent_state, low, high, metrics, after):
+    for row in range(NSTEP, NSTEP + rows):
+        put_coef(row)
+    copies[0].wait()
+    inner = range(NSTEP + 1, NSTEP + rows - 1)
+    one_step(a_ref, b_ref, inner, 0)
+    for copy in copies[1:]:
+        copy.wait()
+    outer = [row for row in range(1, rows + 2 * NSTEP - 1) if row not in inner]
+    for row in outer:
+        if not NSTEP <= row < NSTEP + rows:
+            put_coef(row)
+    one_step(a_ref, b_ref, outer, 0)
+    for step in range(1, NSTEP - 1):
+        source, target = (a_ref, b_ref) if step % 2 == 0 else (b_ref, a_ref)
+        one_step(source, target, range(step + 1, rows + 2 * NSTEP - 1 - step), 0)
+    window = patch_window(meta_ref, columns)[1]
+    done = len(copies)
+    for row in range(rows):
+        one_step(a_ref if NSTEP % 2 else b_ref, last_ref, [NSTEP + row], NSTEP)
+        move(last_ref.at[:, row], out_ref.at[:, row])
+        move(last_ref.at[:, row, :, pl.ds(window, 2 * LANES)], window_ref.at[:, row])
+    for copy in copies[done:]:
+        copy.wait()
+
+
+def parent_run(meta, wave_speed, parent_state, near, far, metrics, after):
     rows, columns = parent_state.shape[1], parent_state.shape[3]
     wide = (FIELDS, rows + 2 * NSTEP, LEVELS, columns)
     return pl.pallas_call(
         parent_kernel,
-        out_shape=(jax.ShapeDtypeStruct(parent_state.shape, F32), TOKEN),
-        in_specs=[SMEM, VMEM, VMEM, VMEM, VMEM, HBM],
-        out_specs=(VMEM, HBM),
+        out_shape=(
+            jax.ShapeDtypeStruct(parent_state.shape, F32),
+            jax.ShapeDtypeStruct((FIELDS, rows, LEVELS, 2 * LANES), F32),
+        ),
+        in_specs=[SMEM, SMEM, HBM, HBM, HBM, VMEM, HBM],
+        out_specs=(HBM, HBM),
         scratch_shapes=[
             pltpu.VMEM(wide, F32),
             pltpu.VMEM(wide, F32),
-            pltpu.VMEM((3, rows + 2 * NSTEP + 4, columns), F32),
+            pltpu.VMEM(parent_state.shape, F32),
+            pltpu.VMEM((2, 2, LEVELS, columns), F32),
             pltpu.VMEM((3, rows + 2 * NSTEP, LEVELS, columns), F32),
+            pltpu.SemaphoreType.DMA((1 + 2 * (FIELDS + 1) + 2 * rows,)),
         ],
         compiler_params=params(),
         cost_estimate=cost(40_000_000, 8_000_000),
         name="parent_run",
-    )(wave_speed, parent_state, low, high, metrics, after)
-
-
-def reorder_kernel(meta_ref, in_ref, after_ref, out_ref, token_ref):
-    def one(index, carry):
-        out_ref[index] = in_ref[meta_ref[META + index]]
+    )(meta, wave_speed, parent_state, near, far, metrics, after)
+
+
+def reorder_kernel(meta_ref, in_ref, after_ref, out_ref, token_ref, sem):
+    def copy(index):
+        return pltpu.make_async_copy(in_ref.at[meta_ref[META + index]], out_ref.at[index], sem)
+
+    def start(index, carry):
+        copy(index).start()
         return carry
 
-    lax.fori_loop(0, in_ref.shape[0], one, 0)
+    lax.fori_loop(0, in_ref.shape[0], start, 0)
+    pltpu.make_async_copy(in_ref, out_ref, sem).wait()
 
 
 def reorder(meta, pieces, after):
@@ -607,21 +651,16 @@
         reorder_kernel,
         out_shape=(jax.ShapeDtypeStruct(pieces.shape, F32), TOKEN),
         in_specs=[SMEM, VMEM, HBM],
-        out_specs=(VMEM, HBM),
+        out_specs=(HBM, HBM),
+        scratch_shapes=[pltpu.SemaphoreType.DMA],
         compiler_params=params(),
         cost_estimate=cost(100_000, 200_000),
         name="reorder",
     )(meta, pieces, after)
 
 
-def insert_kernel(meta_ref, mean_ref, parent_ref, after_ref, out_ref, rows_ref, window_ref, sem):
-    columns = out_ref.shape[3]
-    first = meta_ref[1]
-    window = pl.multiple_of(jnp.minimum(first // LANES * LANES, columns - 2 * LANES), LANES)
-    fetch = pltpu.make_async_copy(
-        parent_ref.at[:, :, :, pl.ds(window, 2 * LANES)], window_ref, sem
-    )
-    fetch.start()
+def insert_kernel(meta_ref, mean_ref, old_ref, parent_ref, out_ref, rows_ref, window_ref, sems):
+    first, window = patch_window(meta_ref, out_ref.shape[3])
     offset = first - window
     lane = iota((LEVELS, LANES), 1)
     for field in range(FIELDS):
@@ -645,47 +684,55 @@
     found = found.reshape(FIELDS, PBX, LEVELS, 2 * LANES)
     wide = iota((LEVELS, 2 * LANES), 1)
     inside = (wide >= offset) & (wide < offset + PBY)
-    fetch.wait()
+    copies = []
     for field in range(FIELDS):
         for row in range(PBX):
-            window_ref[field, row] = jnp.where(inside, found[field, row], window_ref[field, row])
-    store = pltpu.make_async_copy(window_ref, out_ref.at[:, :, :, pl.ds(window, 2 * LANES)], sem)
-    store.start()
-    store.wait()
-
-
-def insert(meta, means, advanced, after):
+            window_ref[field, row] = jnp.where(inside, found[field, row], old_ref[field, row])
+        copies.append(
+            pltpu.make_async_copy(
+                window_ref.at[field],
+                out_ref.at[field, :, :, pl.ds(window, 2 * LANES)],
+                sems.at[field],
+            )
+        )
+        copies[-1].start()
+    for copy in copies:
+        copy.wait()
+
+
+def insert(meta, means, window, advanced):
     return pl.pallas_call(
         insert_kernel,
         out_shape=jax.ShapeDtypeStruct(advanced.shape, F32),
-        in_specs=[SMEM, VMEM, HBM, HBM],
+        in_specs=[SMEM, VMEM, VMEM, HBM],
         out_specs=HBM,
         scratch_shapes=[
             pltpu.VMEM((FIELDS * PBX, LEVELS, LANES), F32),
             pltpu.VMEM((FIELDS, PBX, LEVELS, 2 * LANES), F32),
-            pltpu.SemaphoreType.DMA,
+            pltpu.SemaphoreType.DMA((FIELDS,)),
         ],
-        input_output_aliases={2: 0},
+        input_output_aliases={3: 0},
         compiler_params=params(),
         cost_estimate=cost(4_000_000, 2_000_000),
         name="insert",
-    )(meta, means, advanced, after)
+    )(meta, means, window, advanced)
 
 
 def body(parent_state, nest_state, metrics, wave_speed, nest_patch):
     count = lax.axis_size("tile")
     rows, columns = parent_state.shape[2:]
     per_device = rows // PBX * (columns // PBY)
-    forward = [(i, (i + 1) % count) for i in range(count)]
-    backward = [(target, source) for source, target in forward]
+    near_pairs = [(i, i ^ 1) for i in range(count)]
+    far_pairs = [(i, (i - 1 + 2 * (i % 2)) % count) for i in range(count)]
     parent_state = jnp.transpose(parent_state, (0, 2, 1, 3))
     nest_state = jnp.transpose(nest_state, (0, 1, 3, 2, 4))
 
-    meta, slots, up, down = prepare(nest_patch, parent_state, metrics, per_device)
+    meta, slots, near, far = prepare(nest_patch, parent_state, metrics, per_device)
     recv = lax.all_to_all(slots, "tile", 0, 0, tiled=True)
-    low = lax.ppermute(up, "tile", forward)
-    high = lax.ppermute(down, "tile", backward)
     start = nest_in(nest_state)
+    recv, near, far, start = lax.optimization_barrier((recv, near, far, start))
+    near = lax.ppermute(near, "tile", near_pairs)
+    far = lax.ppermute(far, "tile", far_pairs)
     direct = 15 <= count < 30
     share = 16 if direct else -(-15 * 16 // count)
     final, means, nested = nest_run(meta, wave_speed, recv, start, count if direct else 15)
@@ -694,13 +741,13 @@
         means = jnp.pad(means, ((0, count * share - 15 * 16), (0, 0)))
         means = means.reshape(count, share, LANES)
     spread = lax.all_to_all(means, "tile", 0, 0, tiled=True)
-    advanced, stepped = parent_run(wave_speed, parent_state, low, high, metrics, nested)
-    mixed, ordered = reorder(meta, spread, stepped)
+    nest_next, unpacked = nest_out(final, nested)
+    mixed, ordered = reorder(meta, spread, unpacked)
     returned = lax.all_to_all(mixed, "tile", 0, 0, tiled=True)
-    nest_next, unpacked = nest_out(final, ordered)
+    advanced, window = parent_run(meta, wave_speed, parent_state, near, far, metrics, ordered)
     if not direct:
         returned = returned.reshape(count * share, LANES)[: 15 * 16].reshape(15, 16, LANES)
-    parent_next = insert(meta, returned, advanced, unpacked)
+    parent_next = insert(meta, returned, window, advanced)
     return (jnp.transpose(parent_next, (0, 2, 1, 3)), jnp.transpose(nest_next, (0, 1, 3, 2, 4)))
 
 

time: 63.7 us -> 57.3 us (0.90)
  starting transfers between devices: 25.1 us -> 16.7 us
  waiting for transfers between devices: 5.99 us -> 11.3 us
  Pallas kernels: 28.4 us -> 26.4 us
  local copies, waits for them, and re-layouts: 2.94 us -> 1.57 us
    all_to_all x1, waiting for transfers between devices: 1.36 us -> 6.71 us  [body(): recv = lax.all_to_all(slots, 'tile', 0, 0, tiled=True)]
    all_to_all x1, waiting for transfers between devices: 0.01 us -> 4.62 us  [body(): spread = lax.all_to_all(means, 'tile', 0, 0, tiled=True)]
    all_to_all x1, waiting for transfers between devices: 4.62 us -> 0.01 us  [body(): returned = lax.all_to_all(mixed, 'tile', 0, 0, tiled=True)]
    ppermute x2, starting transfers between devices: 4.49 us -> 1.38 us  [the longest x1 1.37 us: body(): far = lax.ppermute(far, 'tile', far_pairs)]
    all_to_all x1, starting transfers between devices: 7.21 us -> 4.45 us  [body(): spread = lax.all_to_all(means, 'tile', 0, 0, tiled=True)]
    all_to_all x1, starting transfers between devices: 6.01 us -> 3.52 us  [body(): returned = lax.all_to_all(mixed, 'tile', 0, 0, tiled=True)]
    unnamed x12, local copies, waits for them, and re-layouts: 2.94 us -> 1.57 us
    pallas_call x1, Pallas kernels: 2.58 us -> 1.6 us  [insert(): pl.pallas_call(insert_kernel, out_shape=jax.ShapeDtypeStruct(advanced.sha...]
  transfers between devices with their start and end apart: 5 -> 5, of which waited for: 2 -> 2; matrix products, arithmetic and copies ran while one was open for 0% -> 0% of each run, Pallas kernels for 32% -> 37%
where the time goes in v3:
time: 57.3 us; the launch traced here: 56.8 us
  Pallas kernels  26.4 us (46%)
  starting transfers between devices  16.7 us (29%)
  waiting for transfers between devices  11.3 us (20%)
  local copies, waits for them, and re-layouts  1.57 us (3%)
  between operations  0.78 us (1%)
    pallas_call x1, Pallas kernels, nest_run(): pl.pallas_call(nest_kernel, out_shape=(jax.ShapeDtypeStruct(PACKED, F32),...  7.42 us
    all_to_all x1, starting transfers between devices, body(): recv = lax.all_to_all(slots, 'tile', 0, 0, tiled=True)  7.4 us
    pallas_call x1, Pallas kernels, parent_run(): pl.pallas_call(parent_kernel, out_shape=(jax.ShapeDtypeStruct(parent_stat...  7.02 us
    all_to_all x1, waiting for transfers between devices, body(): recv = lax.all_to_all(slots, 'tile', 0, 0, tiled=True)  6.71 us
    all_to_all x1, waiting for transfers between devices, body(): spread = lax.all_to_all(means, 'tile', 0, 0, tiled=True)  4.62 us
    all_to_all x1, starting transfers between devices, body(): spread = lax.all_to_all(means, 'tile', 0, 0, tiled=True)  4.45 us
    pallas_call x1, Pallas kernels, prepare(): pl.pallas_call(functools.partial(prepare_kernel, per_device), out_shape=(...  3.54 us
    all_to_all x1, starting transfers between devices, body(): returned = lax.all_to_all(mixed, 'tile', 0, 0, tiled=True)  3.52 us
  transfers between devices with their start and end apart: 5, of which 2 were waited for; matrix products, arithmetic and copies ran while one was open for 0% of the time, Pallas kernels for 37%

profile of v3, /device:TPU:0, one launch (start us, length us, event | category | flops | bytes accessed | tf_op | source)
XLA Modules:
  0.0 56.8 jit_solution(1226367344053258371)
XLA Ops:
  0.6 3.5 %prepare.1 = (s32[24]{0:T(128)}, f32[16,24,128]{2,1,0:T(8,128)}, f32[22,8,768]{2,1,0:T(8,128)}, f32[22,8,768]{2,1,0:T(8,128)}) custom-call(s32[16]{0:T(128)} %patch_ref.1, f32[5,12,8,768]{3,2,1,0:T(8,128)} %bitcast.4, f32[3,12,768]{2,1,0:T(8,128)} %metrics_ref.3), custom_call_target="tpu_custom_call" | custom-call | flops 4000000 | bytes 4000000 | tf_op jit(solution)/shard_map/prepare/pallas_call | solution.py:187
  4.2 0.0 copy-start.4
  4.2 0.0 copy-start.5
  4.2 7.4 %all-to-all-start = ((f32[16,24,128]{2,1,0:T(8,128)}), f32[16,24,128]{2,1,0:T(8,128)S(1)}, u32[]{:S(2)}, u32[]{:S(2)}) async-start(f32[16,24,128]{2,1,0:T(8,128)} %get-tuple-element.20), calls=%async_computation | async-start | bytes 393216 | tf_op jit(solution)/shard_map/all_to_all | solution.py:731
  11.6 2.3 %nest_in.1.start_ref = f32[5,9,5,8,128]{4,3,2,1,0:T(8,128)S(1)} custom-call(f32[1,5,36,8,144]{4,3,2,1,0:T(8,128)S(1)} %bitcast.6), custom_call_target="tpu_custom_call" | custom-call | flops 8000000 | bytes 6000000 | tf_op jit(solution)/shard_map/nest_in/pallas_call | solution.py:262
  13.9 0.0 copy-start
  13.9 6.7 %all-to-all-done.recv_ref = f32[16,24,128]{2,1,0:T(8,128)S(1)} async-done(((f32[16,24,128]{2,1,0:T(8,128)}), f32[16,24,128]{2,1,0:T(8,128)S(1)}, u32[]{:S(2)}, u32[]{:S(2)}) %all-to-all-start) | async-done | bytes 196640 | tf_op jit(solution)/shard_map/all_to_all | solution.py:731
  20.6 0.0 collective-permute-start
  20.6 1.4 %collective-permute-start.1 = (f32[22,8,768]{2,1,0:T(8,128)}, f32[22,8,768]{2,1,0:T(8,128)}, u32[]{:S(2)}, u32[]{:S(2)}) collective-permute-start(f32[22,8,768]{2,1,0:T(8,128)} %get-tuple-element.31), channel_id=1, source_target_pairs={{0,15},{1,2},{2,1},{3,4},{4,3},{5,6},{6,5},{7,8},{8,7},{9,10},{10,... | collective-permute-start | bytes 1622024 | tf_op jit(solution)/shard_map/ppermute | solution.py:735
  22.0 7.4 %nest_run.1 = (f32[5,9,5,8,128]{4,3,2,1,0:T(8,128)S(1)}, f32[16,16,128]{2,1,0:T(8,128)S(1)}, f32[8,128]{1,0:T(8,128)S(1)}) custom-call(s32[24]{0:T(128)S(1)} %copy-done.4, f32[8]{0:T(128)S(1)} %copy-done.5, f32[16,24,128]{2,1,0:T(8,128)S(1)} %all-to-all-done.recv_ref, f32[5,9,5,8,128]{4,3,2,1,0:T(8,128)S(1)} %nest_in.1.start_ref), custom_call_target="tpu_custom_call" | custom-call | flops 40000000 | bytes 3000000 | tf_op jit(solution)/shard_map/nest_run/pallas_call | solution.py:478
  29.4 0.0 copy-start.3
  29.4 0.6 %copy-done.3 = f32[16,16,128]{2,1,0:T(8,128)} copy-done((f32[16,16,128]{2,1,0:T(8,128)}, f32[16,16,128]{2,1,0:T(8,128)S(1)}, u32[]{:S(2)}) %copy-start.3) | copy-done | bytes 131096
  30.1 4.5 %all-to-all-start.1 = ((f32[16,16,128]{2,1,0:T(8,128)}), f32[16,16,128]{2,1,0:T(8,128)S(1)}, u32[]{:S(2)}, u32[]{:S(2)}) async-start(f32[16,16,128]{2,1,0:T(8,128)} %copy-done.3), calls=%async_computation.1 | async-start | bytes 262144 | tf_op jit(solution)/shard_map/all_to_all | solution.py:743
  34.5 3.3 %nest_out.1 = (f32[1,5,36,8,144]{4,3,2,1,0:T(8,128)}, f32[8,128]{1,0:T(8,128)S(1)}) custom-call(f32[5,9,5,8,128]{4,3,2,1,0:T(8,128)S(1)} %get-tuple-element.26.packed_ref, f32[8,128]{1,0:T(8,128)S(1)} %get-tuple-element.27.after_ref), custom_call_target="tpu_custom_call" | custom-call | flops 8000000 | bytes 6000000 | tf_op jit(solution)/shard_map/nest_out/pallas_call | solution.py:296
  37.8 4.6 %all-to-all-done.1.in_ref = f32[16,16,128]{2,1,0:T(8,128)S(1)} async-done(((f32[16,16,128]{2,1,0:T(8,128)}), f32[16,16,128]{2,1,0:T(8,128)S(1)}, u32[]{:S(2)}, u32[]{:S(2)}) %all-to-all-start.1) | async-done | bytes 131104 | tf_op jit(solution)/shard_map/all_to_all | solution.py:743
  42.5 1.2 %reorder.1 = (f32[16,16,128]{2,1,0:T(8,128)}, f32[8,128]{1,0:T(8,128)S(1)}) custom-call(s32[24]{0:T(128)S(1)} %copy-done.4, f32[16,16,128]{2,1,0:T(8,128)S(1)} %all-to-all-done.1.in_ref, f32[8,128]{1,0:T(8,128)S(1)} %get-tuple-element.28.after_ref), custom_call_target="tpu_custom_call" | custom-call | flops 100000 | bytes 200000 | tf_op jit(solution)/shard_map/reorder/pallas_call | solution.py:650
  43.7 3.5 %all-to-all-start.2 = ((f32[16,16,128]{2,1,0:T(8,128)}), f32[16,16,128]{2,1,0:T(8,128)S(1)}, u32[]{:S(2)}, u32[]{:S(2)}) async-start(f32[16,16,128]{2,1,0:T(8,128)} %get-tuple-element.29), calls=%async_computation.2 | async-start | bytes 262144 | tf_op jit(solution)/shard_map/all_to_all | solution.py:746
  47.2 0.0 collective-permute-done.near_ref
  47.3 0.0 collective-permute-done.1.far_ref
  47.3 0.0 copy-start.2
  47.3 0.9 %copy-done.2 = f32[3,12,768]{2,1,0:T(8,128)S(1)} copy-done((f32[3,12,768]{2,1,0:T(8,128)S(1)}, f32[3,12,768]{2,1,0:T(8,128)}, u32[]{:S(2)}) %copy-start.2) | copy-done | bytes 110616
  48.2 7.0 %parent_run.1 = (f32[5,12,8,768]{3,2,1,0:T(8,128)}, f32[5,12,8,256]{3,2,1,0:T(8,128)S(1)}) custom-call(s32[24]{0:T(128)S(1)} %copy-done.4, f32[8]{0:T(128)S(1)} %copy-done.5, f32[5,12,8,768]{3,2,1,0:T(8,128)S(1)} %bitcast.5, f32[22,8,768]{2,1,0:T(8,128)} %collective-permute-done.near_ref, f32[22,8,768]{2,1,0:T(8,128)} %collective-permute-done.1.far_ref, ...), custom_call_target="tpu_custom_call" | custom-call | flops 40000000 | bytes 8000000 | tf_op jit(solution)/shard_map/parent_run/pallas_call | solution.py:615
  55.2 0.0 all-to-all-done.2.mean_ref
  55.2 1.6 %insert.1 = f32[5,12,8,768]{3,2,1,0:T(8,128)} custom-call(s32[24]{0:T(128)S(1)} %copy-done.4, f32[16,16,128]{2,1,0:T(8,128)S(1)} %all-to-all-done.2.mean_ref, f32[5,12,8,256]{3,2,1,0:T(8,128)S(1)} %get-tuple-element.33.old_ref, f32[5,12,8,768]{3,2,1,0:T(8,128)} %get-tuple-element.34.parent_ref), custom_call_target="tpu_custom_call", output_to_operand_aliasing={{}: (3, {})} | custom-call | flops 4000000 | bytes 2000000 | tf_op jit(solution)/shard_map/insert/pallas_call | solution.py:704
  (5 shorter events, 0.0 us)
Async XLA Ops:
  0.6 11.0 %copy-start.1 = (f32[1,5,8,36,144]{4,2,3,1,0:T(8,128)S(1)}, f32[1,5,8,36,144]{4,2,3,1,0:T(8,128)}, u32[]{:S(2)}) copy-start(f32[1,5,8,36,144]{4,2,3,1,0:T(8,128)} %param.6) | copy-start | bytes 2488324
  4.2 17.8 %copy-start.4 = (s32[24]{0:T(128)S(1)}, s32[24]{0:T(128)}, u32[]{:S(2)}) copy-start(s32[24]{0:T(128)} %get-tuple-element.19.meta_ref) | copy-start | bytes 292
  4.2 17.8 %copy-start.5 = (f32[8]{0:T(128)S(1)}, f32[8]{0:T(128)}, u32[]{:S(2)}) copy-start(f32[8]{0:T(128)} %speed_ref.3) | copy-start | bytes 100
  4.2 16.4 %all-to-all-start = ((f32[16,24,128]{2,1,0:T(8,128)}), f32[16,24,128]{2,1,0:T(8,128)S(1)}, u32[]{:S(2)}, u32[]{:S(2)}) async-start(f32[16,24,128]{2,1,0:T(8,128)} %get-tuple-element.20), calls=%async_computation | async-start | bytes 393216 | tf_op jit(solution)/shard_map/all_to_all | solution.py:731
  13.9 33.4 %copy-start = (f32[5,8,12,768]{3,1,2,0:T(8,128)S(1)}, f32[5,8,12,768]{3,1,2,0:T(8,128)}, u32[]{:S(2)}) copy-start(f32[5,8,12,768]{3,1,2,0:T(8,128)} %param.5) | copy-start | bytes 4423684
  20.6 26.6 %collective-permute-start = (f32[22,8,768]{2,1,0:T(8,128)}, f32[22,8,768]{2,1,0:T(8,128)}, u32[]{:S(2)}, u32[]{:S(2)}) collective-permute-start(f32[22,8,768]{2,1,0:T(8,128)} %get-tuple-element.30), channel_id=1, source_target_pairs={{0,1},{1,0},{2,3},{3,2},{4,5},{5,4},{6,7},{7,6},{8,9},{9,8},{10,11... | collective-permute-start | bytes 1622024 | tf_op jit(solution)/shard_map/ppermute | solution.py:734
  20.6 26.7 %collective-permute-start.1 = (f32[22,8,768]{2,1,0:T(8,128)}, f32[22,8,768]{2,1,0:T(8,128)}, u32[]{:S(2)}, u32[]{:S(2)}) collective-permute-start(f32[22,8,768]{2,1,0:T(8,128)} %get-tuple-element.31), channel_id=1, source_target_pairs={{0,15},{1,2},{2,1},{3,4},{4,3},{5,6},{6,5},{7,8},{8,7},{9,10},{10,... | collective-permute-start | bytes 1622024 | tf_op jit(solution)/shard_map/ppermute | solution.py:735
  29.4 0.7 %copy-start.3 = (f32[16,16,128]{2,1,0:T(8,128)}, f32[16,16,128]{2,1,0:T(8,128)S(1)}, u32[]{:S(2)}) copy-start(f32[16,16,128]{2,1,0:T(8,128)S(1)} %get-tuple-element.25) | copy-start | bytes 393220
  30.1 12.4 %all-to-all-start.1 = ((f32[16,16,128]{2,1,0:T(8,128)}), f32[16,16,128]{2,1,0:T(8,128)S(1)}, u32[]{:S(2)}, u32[]{:S(2)}) async-start(f32[16,16,128]{2,1,0:T(8,128)} %copy-done.3), calls=%async_computation.1 | async-start | bytes 262144 | tf_op jit(solution)/shard_map/all_to_all | solution.py:743
  43.7 11.5 %all-to-all-start.2 = ((f32[16,16,128]{2,1,0:T(8,128)}), f32[16,16,128]{2,1,0:T(8,128)S(1)}, u32[]{:S(2)}, u32[]{:S(2)}) async-start(f32[16,16,128]{2,1,0:T(8,128)} %get-tuple-element.29), calls=%async_computation.2 | async-start | bytes 262144 | tf_op jit(solution)/shard_map/all_to_all | solution.py:746
  47.3 0.9 %copy-start.2 = (f32[3,12,768]{2,1,0:T(8,128)S(1)}, f32[3,12,768]{2,1,0:T(8,128)}, u32[]{:S(2)}) copy-start(f32[3,12,768]{2,1,0:T(8,128)} %metrics_ref.3) | copy-start | bytes 331780

commit v4 on v3

--- a/solution.py
+++ b/solution.py
@@ -133,7 +133,7 @@
     beside = ((after, rows - 1), (before, 0))
     for kind in range(3):
         cells_ref[pl.ds(kind * 16, PBX), :] = metrics_ref[kind, :, pl.ds(window, 2 * LANES)]
-    mets = pick(cells_ref[...], window_matrix(first - window), 3)
+    mets = pick(cells_ref[...], window_matrix(first - window), 2)
     mets = [mets[kind * 16 : kind * 16 + 16] for kind in range(3)]
     lane = iota((16, LANES), 1)
     packed = jnp.where(
@@ -155,7 +155,7 @@
         block = pl.multiple_of(column // LANES * LANES, LANES)
         same = chooser(iota((LANES, LANES), 0) == lax.rem(column, LANES))
         strips = parent_ref[:, :, :, pl.ds(block, LANES)].reshape(FIELDS * PBX * LEVELS, LANES)
-        strips = pick(strips, same, 3)
+        strips = pick(strips, same, 2)
         for field in range(FIELDS):
             for row in range(PBX):
                 at = (field * PBX + row) * LEVELS
@@ -168,7 +168,7 @@
         first, window = place(block)
         lines = parent_ref[:, row, :, pl.ds(window, 2 * LANES)]
         lines = lines.reshape(FIELDS * LEVELS, 2 * LANES)
-        found = pick(lines, window_matrix(first - window), 3)
+        found = pick(lines, window_matrix(first - window), 2)
         found = [found[field * LEVELS : (field + 1) * LEVELS] for field in range(FIELDS)]
         for pair in range(2):
             mine_ref[1 + side, pl.ds(8 * pair, 8), :] = jnp.where(
@@ -354,7 +354,7 @@
     rows = chooser(coarse_row == iota((64, PBX), 1))
     both = jnp.concatenate([source[8:20], last], axis=1)
     expanded = None
-    for term in range(3):
+    for term in range(2):
         part = both.astype(BF16)
         piece = jnp.dot(rows, part, preferred_element_type=F32)
         expanded = piece if expanded is None else expanded + piece
@@ -471,7 +471,14 @@
                     shift = GROUPS * (coarse - 8 * half - at) % LANES
                     piece = pltpu.roll(totals[row], shift, 1) if shift else totals[row]
                     mean = piece if mean is None else jnp.where(chunk == coarse % 8, piece, mean)
-                mean_ref[field * 3 + third, pl.ds(8 * half, 8), :] = mean
+                at = 3 * (field * 3 + third)
+                if half == 0:
+                    mean_ref[at] = mean[:4]
+                    mean_ref[at + 1] = mean[4:]
+                else:
+                    mean_ref[at + 2] = jnp.where(
+                        lane[:4] < LANES // 2, mean[:4], pltpu.roll(mean, LANES // 2, 1)[4:]
+                    )
 
 def nest_run(meta, wave_speed, recv, start, pieces):
     padded = (FIELDS, COLS + 2, ROWS + 2, 8, LANES)
@@ -479,7 +486,7 @@
         nest_kernel,
         out_shape=(
             jax.ShapeDtypeStruct(PACKED, F32),
-            jax.ShapeDtypeStruct((pieces, 16, LANES), F32),
+            jax.ShapeDtypeStruct((pieces * 3, 4, LANES), F32),
             TOKEN,
         ),
         in_specs=[SMEM, SMEM, VMEM, VMEM],
@@ -635,14 +642,15 @@
 
 
 def reorder_kernel(meta_ref, in_ref, after_ref, out_ref, token_ref, sem):
-    def copy(index):
-        return pltpu.make_async_copy(in_ref.at[meta_ref[META + index]], out_ref.at[index], sem)
+    count = meta_ref.shape[0] - META
+    size = in_ref.shape[0] // count
 
     def start(index, carry):
-        copy(index).start()
+        source = in_ref.at[pl.ds(meta_ref[META + index] * size, size)]
+        pltpu.make_async_copy(source, out_ref.at[pl.ds(index * size, size)], sem).start()
         return carry
 
-    lax.fori_loop(0, in_ref.shape[0], start, 0)
+    lax.fori_loop(0, count, start, 0)
     pltpu.make_async_copy(in_ref, out_ref, sem).wait()
 
 
@@ -664,10 +672,16 @@
     offset = first - window
     lane = iota((LEVELS, LANES), 1)
     for field in range(FIELDS):
+        upper, lower = [], []
+        for third in range(3):
+            at = 3 * (field * 3 + third)
+            tail = mean_ref[at + 2]
+            upper.append(jnp.concatenate([mean_ref[at], mean_ref[at + 1]], axis=0))
+            lower.append(jnp.concatenate([tail, pltpu.roll(tail, LANES // 2, 1)], axis=0))
         for row in range(PBX):
             turned = []
             for third in range(3):
-                piece = mean_ref[field * 3 + third, pl.ds(row // 8 * 8, 8), :]
+                piece = upper[third] if row < 8 else lower[third]
                 shift = GROUPS * (third - row % 8) % LANES
                 turned.append(pltpu.roll(piece, shift, 1) if shift else piece)
             rows_ref[field * PBX + row] = jnp.where(
@@ -733,12 +747,12 @@
     recv, near, far, start = lax.optimization_barrier((recv, near, far, start))
     near = lax.ppermute(near, "tile", near_pairs)
     far = lax.ppermute(far, "tile", far_pairs)
-    direct = 15 <= count < 30
-    share = 16 if direct else -(-15 * 16 // count)
+    direct = 15 <= count <= 16
+    share = -(-15 * PBX // count)
     final, means, nested = nest_run(meta, wave_speed, recv, start, count if direct else 15)
     if not direct:
-        means = means.reshape(15 * 16, LANES)
-        means = jnp.pad(means, ((0, count * share - 15 * 16), (0, 0)))
+        means = means.reshape(15 * PBX, LANES)
+        means = jnp.pad(means, ((0, count * share - 15 * PBX), (0, 0)))
         means = means.reshape(count, share, LANES)
     spread = lax.all_to_all(means, "tile", 0, 0, tiled=True)
     nest_next, unpacked = nest_out(final, nested)
@@ -746,7 +760,7 @@
     returned = lax.all_to_all(mixed, "tile", 0, 0, tiled=True)
     advanced, window = parent_run(meta, wave_speed, parent_state, near, far, metrics, ordered)
     if not direct:
-        returned = returned.reshape(count * share, LANES)[: 15 * 16].reshape(15, 16, LANES)
+        returned = returned.reshape(count * share, LANES)[: 15 * PBX].reshape(45, 4, LANES)
     parent_next = insert(meta, returned, window, advanced)
     return (jnp.transpose(parent_next, (0, 2, 1, 3)), jnp.transpose(nest_next, (0, 1, 3, 2, 4)))
 

time: 57.3 us -> 56.7 us (0.990)
  transfers between devices with their start and end apart: 5 -> 5, of which waited for: 2 -> 2; matrix products, arithmetic and copies ran while one was open for 0% -> 0% of each run, Pallas kernels for 37% -> 38%
where the time goes in v4:
time: 56.7 us; the launch traced here: 56.2 us
  Pallas kernels  26.4 us (47%)
  starting transfers between devices  16.7 us (29%)
  waiting for transfers between devices  10.8 us (19%)
  local copies, waits for them, and re-layouts  1.55 us (3%)
  between operations  0.78 us (1%)
    pallas_call x1, Pallas kernels, nest_run(): pl.pallas_call(nest_kernel, out_shape=(jax.ShapeDtypeStruct(PACKED, F32),...  7.4 us
    all_to_all x1, starting transfers between devices, body(): recv = lax.all_to_all(slots, 'tile', 0, 0, tiled=True)  7.39 us
    pallas_call x1, Pallas kernels, parent_run(): pl.pallas_call(parent_kernel, out_shape=(jax.ShapeDtypeStruct(parent_stat...  7.02 us
    all_to_all x1, waiting for transfers between devices, body(): recv = lax.all_to_all(slots, 'tile', 0, 0, tiled=True)  6.71 us
    all_to_all x1, starting transfers between devices, body(): spread = lax.all_to_all(means, 'tile', 0, 0, tiled=True)  4.45 us
    all_to_all x1, waiting for transfers between devices, body(): spread = lax.all_to_all(means, 'tile', 0, 0, tiled=True)  4.09 us
    all_to_all x1, starting transfers between devices, body(): returned = lax.all_to_all(mixed, 'tile', 0, 0, tiled=True)  3.52 us
    pallas_call x1, Pallas kernels, prepare(): pl.pallas_call(functools.partial(prepare_kernel, per_device), out_shape=(...  3.46 us
  transfers between devices with their start and end apart: 5, of which 2 were waited for; matrix products, arithmetic and copies ran while one was open for 0% of the time, Pallas kernels for 38%

profile of v4, /device:TPU:0, one launch (start us, length us, event | category | flops | bytes accessed | tf_op | source)
XLA Modules:
  0.0 56.2 jit_solution(9798300951737964446)
XLA Ops:
  0.6 3.5 %prepare.1 = (s32[24]{0:T(128)}, f32[16,24,128]{2,1,0:T(8,128)}, f32[22,8,768]{2,1,0:T(8,128)}, f32[22,8,768]{2,1,0:T(8,128)}) custom-call(s32[16]{0:T(128)} %patch_ref.1, f32[5,12,8,768]{3,2,1,0:T(8,128)} %bitcast.4, f32[3,12,768]{2,1,0:T(8,128)} %metrics_ref.3), custom_call_target="tpu_custom_call" | custom-call | flops 4000000 | bytes 4000000 | tf_op jit(solution)/shard_map/prepare/pallas_call | solution.py:187
  4.1 0.0 copy-start.5
  4.1 7.4 %all-to-all-start = ((f32[16,24,128]{2,1,0:T(8,128)}), f32[16,24,128]{2,1,0:T(8,128)S(1)}, u32[]{:S(2)}, u32[]{:S(2)}) async-start(f32[16,24,128]{2,1,0:T(8,128)} %get-tuple-element.20), calls=%async_computation | async-start | bytes 393216 | tf_op jit(solution)/shard_map/all_to_all | solution.py:745
  11.5 0.0 copy-done.1
  11.5 2.3 %nest_in.1.start_ref = f32[5,9,5,8,128]{4,3,2,1,0:T(8,128)S(1)} custom-call(f32[1,5,36,8,144]{4,3,2,1,0:T(8,128)S(1)} %bitcast.6), custom_call_target="tpu_custom_call" | custom-call | flops 8000000 | bytes 6000000 | tf_op jit(solution)/shard_map/nest_in/pallas_call | solution.py:262
  13.8 0.0 copy-start
  13.8 6.7 %all-to-all-done.recv_ref = f32[16,24,128]{2,1,0:T(8,128)S(1)} async-done(((f32[16,24,128]{2,1,0:T(8,128)}), f32[16,24,128]{2,1,0:T(8,128)S(1)}, u32[]{:S(2)}, u32[]{:S(2)}) %all-to-all-start) | async-done | bytes 196640 | tf_op jit(solution)/shard_map/all_to_all | solution.py:745
  20.5 0.0 collective-permute-start
  20.5 1.4 %collective-permute-start.1 = (f32[22,8,768]{2,1,0:T(8,128)}, f32[22,8,768]{2,1,0:T(8,128)}, u32[]{:S(2)}, u32[]{:S(2)}) collective-permute-start(f32[22,8,768]{2,1,0:T(8,128)} %get-tuple-element.31), channel_id=1, source_target_pairs={{0,15},{1,2},{2,1},{3,4},{4,3},{5,6},{6,5},{7,8},{8,7},{9,10},{10,... | collective-permute-start | bytes 1622024 | tf_op jit(solution)/shard_map/ppermute | solution.py:749
  21.9 0.0 copy-done.5
  21.9 7.4 %nest_run.1 = (f32[5,9,5,8,128]{4,3,2,1,0:T(8,128)S(1)}, f32[48,4,128]{2,1,0:T(4,128)S(1)}, f32[8,128]{1,0:T(8,128)S(1)}) custom-call(s32[24]{0:T(128)S(1)} %copy-done.4, f32[8]{0:T(128)S(1)} %copy-done.5, f32[16,24,128]{2,1,0:T(8,128)S(1)} %all-to-all-done.recv_ref, f32[5,9,5,8,128]{4,3,2,1,0:T(8,128)S(1)} %nest_in.1.start_ref), custom_call_target="tpu_custom_call" | custom-call | flops 40000000 | bytes 3000000 | tf_op jit(solution)/shard_map/nest_run/pallas_call | solution.py:485
  29.3 0.6 %copy-done.3 = f32[48,4,128]{2,1,0:T(4,128)} copy-done((f32[48,4,128]{2,1,0:T(4,128)}, f32[48,4,128]{2,1,0:T(4,128)S(1)}, u32[]{:S(2)}) %copy-start.3) | copy-done | bytes 98328
  29.9 4.5 %all-to-all-start.1 = ((f32[48,4,128]{2,1,0:T(4,128)}), f32[48,4,128]{2,1,0:T(4,128)S(1)}, u32[]{:S(2)}, u32[]{:S(2)}) async-start(f32[48,4,128]{2,1,0:T(4,128)} %copy-done.3), calls=%async_computation.1 | async-start | bytes 196608 | tf_op jit(solution)/shard_map/all_to_all | solution.py:757
  34.4 3.3 %nest_out.1 = (f32[1,5,36,8,144]{4,3,2,1,0:T(8,128)}, f32[8,128]{1,0:T(8,128)S(1)}) custom-call(f32[5,9,5,8,128]{4,3,2,1,0:T(8,128)S(1)} %get-tuple-element.26.packed_ref, f32[8,128]{1,0:T(8,128)S(1)} %get-tuple-element.27.after_ref), custom_call_target="tpu_custom_call" | custom-call | flops 8000000 | bytes 6000000 | tf_op jit(solution)/shard_map/nest_out/pallas_call | solution.py:296
  37.7 4.1 %all-to-all-done.1.in_ref = f32[48,4,128]{2,1,0:T(4,128)S(1)} async-done(((f32[48,4,128]{2,1,0:T(4,128)}), f32[48,4,128]{2,1,0:T(4,128)S(1)}, u32[]{:S(2)}, u32[]{:S(2)}) %all-to-all-start.1) | async-done | bytes 98336 | tf_op jit(solution)/shard_map/all_to_all | solution.py:757
  41.8 1.2 %reorder.1 = (f32[48,4,128]{2,1,0:T(4,128)}, f32[8,128]{1,0:T(8,128)S(1)}) custom-call(s32[24]{0:T(128)S(1)} %copy-done.4, f32[48,4,128]{2,1,0:T(4,128)S(1)} %all-to-all-done.1.in_ref, f32[8,128]{1,0:T(8,128)S(1)} %get-tuple-element.28.after_ref), custom_call_target="tpu_custom_call" | custom-call | flops 100000 | bytes 200000 | tf_op jit(solution)/shard_map/reorder/pallas_call | solution.py:658
  43.1 3.5 %all-to-all-start.2 = ((f32[48,4,128]{2,1,0:T(4,128)}), f32[48,4,128]{2,1,0:T(4,128)S(1)}, u32[]{:S(2)}, u32[]{:S(2)}) async-start(f32[48,4,128]{2,1,0:T(4,128)} %get-tuple-element.29), calls=%async_computation.2 | async-start | bytes 196608 | tf_op jit(solution)/shard_map/all_to_all | solution.py:760
  46.6 0.0 collective-permute-done.near_ref
  46.6 0.0 collective-permute-done.1.far_ref
  46.6 0.0 copy-start.2
  46.6 0.9 %copy-done.2 = f32[3,12,768]{2,1,0:T(8,128)S(1)} copy-done((f32[3,12,768]{2,1,0:T(8,128)S(1)}, f32[3,12,768]{2,1,0:T(8,128)}, u32[]{:S(2)}) %copy-start.2) | copy-done | bytes 110616
  47.5 7.0 %parent_run.1 = (f32[5,12,8,768]{3,2,1,0:T(8,128)}, f32[5,12,8,256]{3,2,1,0:T(8,128)S(1)}) custom-call(s32[24]{0:T(128)S(1)} %copy-done.4, f32[8]{0:T(128)S(1)} %copy-done.5, f32[5,12,8,768]{3,2,1,0:T(8,128)S(1)} %bitcast.5, f32[22,8,768]{2,1,0:T(8,128)} %collective-permute-done.near_ref, f32[22,8,768]{2,1,0:T(8,128)} %collective-permute-done.1.far_ref, ...), custom_call_target="tpu_custom_call" | custom-call | flops 40000000 | bytes 8000000 | tf_op jit(solution)/shard_map/parent_run/pallas_call | solution.py:622
  54.6 0.0 all-to-all-done.2.mean_ref
  54.6 1.7 %insert.1 = f32[5,12,8,768]{3,2,1,0:T(8,128)} custom-call(s32[24]{0:T(128)S(1)} %copy-done.4, f32[48,4,128]{2,1,0:T(4,128)S(1)} %all-to-all-done.2.mean_ref, f32[5,12,8,256]{3,2,1,0:T(8,128)S(1)} %get-tuple-element.33.old_ref, f32[5,12,8,768]{3,2,1,0:T(8,128)} %get-tuple-element.34.parent_ref), custom_call_target="tpu_custom_call", output_to_operand_aliasing={{}: (3, {})} | custom-call | flops 4000000 | bytes 2000000 | tf_op jit(solution)/shard_map/insert/pallas_call | solution.py:718
  (5 shorter events, 0.0 us)
Async XLA Ops:
  0.6 10.9 %copy-start.1 = (f32[1,5,8,36,144]{4,2,3,1,0:T(8,128)S(1)}, f32[1,5,8,36,144]{4,2,3,1,0:T(8,128)}, u32[]{:S(2)}) copy-start(f32[1,5,8,36,144]{4,2,3,1,0:T(8,128)} %param.6) | copy-start | bytes 2488324
  4.1 17.8 %copy-start.4 = (s32[24]{0:T(128)S(1)}, s32[24]{0:T(128)}, u32[]{:S(2)}) copy-start(s32[24]{0:T(128)} %get-tuple-element.19.meta_ref) | copy-start | bytes 292
  4.1 17.8 %copy-start.5 = (f32[8]{0:T(128)S(1)}, f32[8]{0:T(128)}, u32[]{:S(2)}) copy-start(f32[8]{0:T(128)} %speed_ref.3) | copy-start | bytes 100
  4.1 16.4 %all-to-all-start = ((f32[16,24,128]{2,1,0:T(8,128)}), f32[16,24,128]{2,1,0:T(8,128)S(1)}, u32[]{:S(2)}, u32[]{:S(2)}) async-start(f32[16,24,128]{2,1,0:T(8,128)} %get-tuple-element.20), calls=%async_computation | async-start | bytes 393216 | tf_op jit(solution)/shard_map/all_to_all | solution.py:745
  13.8 32.8 %copy-start = (f32[5,8,12,768]{3,1,2,0:T(8,128)S(1)}, f32[5,8,12,768]{3,1,2,0:T(8,128)}, u32[]{:S(2)}) copy-start(f32[5,8,12,768]{3,1,2,0:T(8,128)} %param.5) | copy-start | bytes 4423684
  20.5 26.1 %collective-permute-start = (f32[22,8,768]{2,1,0:T(8,128)}, f32[22,8,768]{2,1,0:T(8,128)}, u32[]{:S(2)}, u32[]{:S(2)}) collective-permute-start(f32[22,8,768]{2,1,0:T(8,128)} %get-tuple-element.30), channel_id=1, source_target_pairs={{0,1},{1,0},{2,3},{3,2},{4,5},{5,4},{6,7},{7,6},{8,9},{9,8},{10,11... | collective-permute-start | bytes 1622024 | tf_op jit(solution)/shard_map/ppermute | solution.py:748
  20.5 26.1 %collective-permute-start.1 = (f32[22,8,768]{2,1,0:T(8,128)}, f32[22,8,768]{2,1,0:T(8,128)}, u32[]{:S(2)}, u32[]{:S(2)}) collective-permute-start(f32[22,8,768]{2,1,0:T(8,128)} %get-tuple-element.31), channel_id=1, source_target_pairs={{0,15},{1,2},{2,1},{3,4},{4,3},{5,6},{6,5},{7,8},{8,7},{9,10},{10,... | collective-permute-start | bytes 1622024 | tf_op jit(solution)/shard_map/ppermute | solution.py:749
  29.3 0.6 %copy-start.3 = (f32[48,4,128]{2,1,0:T(4,128)}, f32[48,4,128]{2,1,0:T(4,128)S(1)}, u32[]{:S(2)}) copy-start(f32[48,4,128]{2,1,0:T(4,128)S(1)} %get-tuple-element.25) | copy-start | bytes 294916
  29.9 11.9 %all-to-all-start.1 = ((f32[48,4,128]{2,1,0:T(4,128)}), f32[48,4,128]{2,1,0:T(4,128)S(1)}, u32[]{:S(2)}, u32[]{:S(2)}) async-start(f32[48,4,128]{2,1,0:T(4,128)} %copy-done.3), calls=%async_computation.1 | async-start | bytes 196608 | tf_op jit(solution)/shard_map/all_to_all | solution.py:757
  43.1 11.5 %all-to-all-start.2 = ((f32[48,4,128]{2,1,0:T(4,128)}), f32[48,4,128]{2,1,0:T(4,128)S(1)}, u32[]{:S(2)}, u32[]{:S(2)}) async-start(f32[48,4,128]{2,1,0:T(4,128)} %get-tuple-element.29), calls=%async_computation.2 | async-start | bytes 196608 | tf_op jit(solution)/shard_map/all_to_all | solution.py:760
  46.6 0.9 %copy-start.2 = (f32[3,12,768]{2,1,0:T(8,128)S(1)}, f32[3,12,768]{2,1,0:T(8,128)}, u32[]{:S(2)}) copy-start(f32[3,12,768]{2,1,0:T(8,128)} %metrics_ref.3) | copy-start | bytes 331780
